TPU v7x, 256 devices: a whole 4x4x8 slice. The times are simulated.
256 devices in a mesh: seq: 64 (over y, z, core), head: 4 (over x).
Axes of the slice: x: 4, y: 4, z: 8, core: 2. Of those that a mesh axis runs over, the one named last changes fastest.
Arguments:
- queries: bfloat16 [49152, 2560], P('seq', 'head'), may hold values from -12 to 12
- keys: bfloat16 [49152, 2560], P('seq', 'head'), may hold values from -6 to 6
- values: bfloat16 [49152, 2560], P('seq', 'head'), may hold values from -6 to 6
- w_out: bfloat16 [2560, 5120], P('head'), may hold values from -0.125 to 0.125
- selected: int32 [768, 16], P('seq'), may hold values from 0 to 767, as said below
- home: int32 [768], replicated, may hold values from 0 to 767, as said below
Outputs:
- projected: bfloat16 [49152, 5120], P('seq', 'head')
Inputs may be any that keep to these rules, and one draw needn't show every extreme that they name: `selected`: every row names 16 different cubes. Taken together, the rows of the 12 slots of one index of seq name at most 1 different cubes whose slots lie on any one index of seq, and exactly 1 for some index. `home`: A permutation: every slot holds exactly one cube; slot j lies on index j // 12 of seq.
All inputs are finite; a program needn't handle non-finite values.
Results may differ from a plain program's by a relative error of at most 0.0057.
Values may be sent and summed in bfloat16 or wider, within the bound.
No kernel may reach another device: no remote copies, remote signals or barrier semaphores. Data moves between devices by JAX's collectives and lax.ppermute only.
A program may use at most 192 MiB of HBM per device.

v0:
```python
import jax
import jax.numpy as jnp
from jax import lax
from jax.sharding import PartitionSpec as P

HEAD_DIM = 128
CUBE = 64
SEL = 16


def picks_from(marked, capacity):
    ranked = jnp.cumsum(marked, axis=1)
    levels = jnp.arange(1, capacity + 1, dtype=jnp.int32)
    matches = (marked[:, :, None] == 1) & (ranked[:, :, None] == levels[None, None, :])
    column = jnp.arange(marked.shape[1], dtype=jnp.int32)
    picked = jnp.sum(jnp.where(matches, column[None, :, None], 0), axis=1)
    return (picked, ranked)


def per_device(queries, keys, values, w_out, selected, home):
    token_rows, width = queries.shape
    cubes_here = token_rows // CUBE
    devices = lax.axis_size("seq")
    capacity = max(1, SEL // devices)
    total_cubes = cubes_here * devices
    heads_here = width // HEAD_DIM
    catalog = jnp.arange(total_cubes, dtype=jnp.int32)
    slot_of = jnp.sum(
        jnp.where(selected[:, :, None] == catalog[None, None, :], home[None, None, :], 0), axis=2
    )
    onehot = slot_of.reshape(-1)[:, None] == catalog[None, :]
    marked = jnp.any(onehot, axis=0).astype(jnp.int32).reshape(devices, cubes_here)
    wanted, ranked = picks_from(marked, capacity)
    owner_ids = jnp.arange(devices, dtype=jnp.int32)
    position_table = (owner_ids[:, None] * capacity + ranked - 1).reshape(total_cubes)
    positions = jnp.sum(jnp.where(onehot, position_table[None, :], 0), axis=1).reshape(
        cubes_here, SEL
    )
    asked = lax.all_to_all(wanted, "seq", split_axis=0, concat_axis=0, tiled=True)
    key_blocks = keys.reshape(cubes_here, CUBE, width)
    value_blocks = values.reshape(cubes_here, CUBE, width)
    outgoing_keys = key_blocks[asked]
    outgoing_values = value_blocks[asked]
    arrived_keys, arrived_values = (
        lax.all_to_all(outgoing_keys, "seq", split_axis=0, concat_axis=0, tiled=True),
        lax.all_to_all(outgoing_values, "seq", split_axis=0, concat_axis=0, tiled=True),
    )
    flat_keys = arrived_keys.reshape(devices * capacity, CUBE, heads_here, HEAD_DIM)
    flat_values = arrived_values.reshape(devices * capacity, CUBE, heads_here, HEAD_DIM)
    chosen_keys = flat_keys[positions].reshape(cubes_here, SEL * CUBE, heads_here, HEAD_DIM)
    chosen_values = flat_values[positions].reshape(cubes_here, SEL * CUBE, heads_here, HEAD_DIM)
    query_blocks = queries.reshape(cubes_here, CUBE, heads_here, HEAD_DIM)
    scores = jnp.einsum(
        "bqhd,bkhd->bhqk", query_blocks, chosen_keys, preferred_element_type=jnp.float32
    ) * HEAD_DIM ** (-0.5)
    peak = jnp.max(scores, axis=3, keepdims=True)
    raised = jnp.exp(scores - peak)
    probs = (raised / jnp.sum(raised, axis=3, keepdims=True)).astype(jnp.bfloat16)
    attended = jnp.einsum(
        "bhqk,bkhd->bqhd", probs, chosen_values, preferred_element_type=jnp.float32
    )
    attended = attended.astype(jnp.bfloat16).reshape(token_rows, width)
    partial_out = jnp.dot(attended, w_out, preferred_element_type=jnp.float32)
    combined = lax.psum_scatter(partial_out, "head", scatter_dimension=1, tiled=True)
    return combined.astype(jnp.bfloat16)


def solution(mesh):
    in_specs = (
        P("seq", "head"),
        P("seq", "head"),
        P("seq", "head"),
        P("head", None),
        P("seq", None),
        P(),
    )
    out_specs = P("seq", "head")
    return jax.shard_map(
        per_device, mesh=mesh, in_specs=in_specs, out_specs=out_specs, check_vma=False
    )
```

profile of v0, /device:TPU:1, one launch (start us, length us, event | category | flops | bytes accessed | tf_op | source)
XLA Modules:
  0.0 490.6 jit_solution(12982867696469681314)
XLA Ops:
  6.5 0.0 copy-start
  6.5 0.0 copy-start.2
  6.5 1.2 select_reduce_fusion.1
  7.8 0.1 eq.59
  7.8 0.2 fusion.22
  8.0 0.1 reshape.145
  8.1 0.1 eq.64
  8.2 0.2 reduce_window_sum.11
  8.4 0.1 select_reduce_fusion.2
  8.5 0.1 copy.36
  8.6 22.2 %all_to_all.19 = s32[64,1,1]{2,1,0:T(1,128)S(1)} all-to-all(s32[64,1,1]{2,1,0:T(1,128)S(1)} %copy.36), channel_id=1, replica_groups=mesh['seq'=64,'head'=4] {'seq'}, dimensions={0} | all-to-all | bytes 512 | tf_op jit(solution)/shard_map/all_to_all | solution.py:39
  30.9 1.2 fusion.23
  32.1 0.0 copy-done
  32.1 3.5 gather_fusion.2
  35.6 0.0 copy-start.3
  35.6 5.9 %all-to-all-start.2 = ((bf16[64,1,64,640]{3,2,1,0:T(8,128)(2,1)}), bf16[64,1,64,640]{3,2,1,0:T(8,128)(2,1)}, u32[]{:S(2)}, u32[]{:S(2)}) async-start(bf16[64,1,64,640]{3,2,1,0:T(8,128)(2,1)} %bitcast.41), calls=%async_computation.2 | async-start | bytes 10485760 | tf_op jit(solution)/shard_map/all_to_all | solution.py:45
  41.5 0.0 copy-done.2
  41.5 3.5 gather_fusion
  45.0 114.9 %all-to-all-done.2 = bf16[64,1,64,640]{3,2,1,0:T(8,128)(2,1)} async-done(((bf16[64,1,64,640]{3,2,1,0:T(8,128)(2,1)}), bf16[64,1,64,640]{3,2,1,0:T(8,128)(2,1)}, u32[]{:S(2)}, u32[]{:S(2)}) %all-to-all-start.2) | async-done | bytes 5242912 | tf_op jit(solution)/shard_map/all_to_all | solution.py:45
  159.9 6.0 %all-to-all-start.1 = ((bf16[64,1,64,640]{3,2,1,0:T(8,128)(2,1)}), bf16[64,1,64,640]{3,2,1,0:T(8,128)(2,1)}, u32[]{:S(2)}, u32[]{:S(2)}) async-start(bf16[64,1,64,640]{3,2,1,0:T(8,128)(2,1)} %bitcast.40), calls=%async_computation.1 | async-start | bytes 10485760 | tf_op jit(solution)/shard_map/all_to_all | solution.py:46
  165.9 0.2 reduce-scatter.2.cloned.1.call-start
  166.2 0.1 sub.15
  166.3 0.2 select_reduce_fusion
  166.5 0.1 reshape.138
  166.6 0.1 reshape.156
  166.7 0.0 copy-done.3
  166.7 1.1 reshape.143
  167.8 12.6 %reshape.141 = bf16[64,64,5,128]{3,2,1,0:T(8,128)(2,1)} reshape(bf16[64,1,64,640]{3,2,1,0:T(8,128)(2,1)} %all-to-all-done.2) | data formatting | bytes 10485760 | tf_op jit(solution)/shard_map/reshape | solution.py:48
  180.5 14.7 %gather_fusion.3 = bf16[192,64,5,128]{3,2,1,0:T(8,128)(2,1)} fusion(bf16[64,64,5,128]{3,2,1,0:T(8,128)(2,1)} %reshape.141, s32[1024]{0:T(1024)S(1)} %pad_clamp_fusion), kind=kCustom, calls=%fused_computation.3 | custom fusion | bytes 31458048 | tf_op jit(solution)/shard_map/gather | solution.py:50
  195.2 16.5 %fusion.3 = f32[12,5,1024,64]{2,3,1,0:T(8,128)} fusion(bf16[12,1024,5,128]{3,2,1,0:T(8,128)(2,1)} %bitcast.37, bf16[12,64,5,128]{3,2,1,0:T(8,128)(2,1)S(1)} %reshape.143), kind=kOutput, calls=%fused_computation.9 | convolution fusion | flops 1006632960 | bytes 32440320 | tf_op jit(solution)/shard_map/bqhd,bkhd->bhqk/dot_general | solution.py:53
  211.7 17.6 %fusion.26 = (f32[12,5,64]{2,1,0:T(8,128)S(1)}, f32[12,5,64,1024]{3,2,1,0:T(8,128)}) fusion(f32[12,5,1024,64]{2,3,1,0:T(8,128)} %fusion.3), kind=kOutput, calls=%fused_computation.39 | output fusion | flops 15729663 | bytes 31472640 | tf_op jit(solution)/shard_map/sub | solution.py:57
  229.3 55.0 %all-to-all-done.1 = bf16[64,1,64,640]{3,2,1,0:T(8,128)(2,1)} async-done(((bf16[64,1,64,640]{3,2,1,0:T(8,128)(2,1)}), bf16[64,1,64,640]{3,2,1,0:T(8,128)(2,1)}, u32[]{:S(2)}, u32[]{:S(2)}) %all-to-all-start.1) | async-done | bytes 5242912 | tf_op jit(solution)/shard_map/all_to_all | solution.py:46
  284.3 12.6 %reshape.137 = bf16[64,64,5,128]{3,2,1,0:T(8,128)(2,1)} reshape(bf16[64,1,64,640]{3,2,1,0:T(8,128)(2,1)} %all-to-all-done.1) | data formatting | bytes 10485760 | tf_op jit(solution)/shard_map/reshape | solution.py:49
  296.9 14.8 %gather_fusion.1 = bf16[192,64,5,128]{3,2,1,0:T(8,128)(2,1)} fusion(bf16[64,64,5,128]{3,2,1,0:T(8,128)(2,1)} %reshape.137, s32[1024]{0:T(1024)S(1)} %pad_clamp_fusion), kind=kCustom, calls=%fused_computation.1 | custom fusion | bytes 31458048 | tf_op jit(solution)/shard_map/gather | solution.py:51
  311.7 16.5 %fusion.15 = bf16[12,64,5,128]{3,1,2,0:T(8,128)(2,1)S(1)} fusion(bf16[12,1024,5,128]{3,2,1,0:T(8,128)(2,1)} %bitcast.39, f32[12,5,64,1024]{3,2,1,0:T(8,128)} %get-tuple-element.8, f32[12,5,64]{2,1,0:T(8,128)S(1)} %get-tuple-element.7), kind=kOutput, calls=%fused_computation.18 | convolution fusion | flops 1014988800 | bytes 32455680 | tf_op jit(solution)/shard_map/bhqk,bkhd->bqhd/dot_general | solution.py:59
  328.2 0.8 copy.42
  328.9 0.0 copy-start.1
  328.9 12.1 %fusion.18 = f32[768,5120]{1,0:T(8,128)} fusion(bf16[640,5120]{1,0:T(8,128)(2,1)} %param.9, bf16[96,8,5,128]{3,2,1,0:T(8,128)(2,1)S(1)} %bitcast.42), kind=kOutput, calls=%fused_computation.19 | convolution fusion | flops 5033164800 | bytes 23265280 | tf_op jit(solution)/shard_map/dot_general | solution.py:63
  341.0 0.0 reduce-scatter.2.cloned.1.call-update
  341.0 139.2 %reduce-scatter.2.cloned.1.call-done = f32[768,1280]{1,0:T(8,128)} async-done(((f32[768,5120]{1,0:T(8,128)}), f32[768,1280]{1,0:T(8,128)}) %reduce-scatter.2.cloned.1.call-update) | async-done | bytes 3932176 | tf_op jit(solution)/shard_map/reduce_scatter | solution.py:64
  480.2 3.6 convert_element_type.36
  483.8 0.0 copy-done.1
  (5 shorter events, 0.0 us)
Async XLA Ops:
  6.5 25.6 %copy-start = (bf16[768,640]{1,0:T(8,128)(2,1)S(1)}, bf16[768,640]{1,0:T(8,128)(2,1)}, u32[]{:S(2)}) copy-start(bf16[768,640]{1,0:T(8,128)(2,1)} %param.7) | copy-start | bytes 2949124
  6.5 34.9 %copy-start.2 = (bf16[768,640]{1,0:T(8,128)(2,1)S(1)}, bf16[768,640]{1,0:T(8,128)(2,1)}, u32[]{:S(2)}) copy-start(bf16[768,640]{1,0:T(8,128)(2,1)} %param.8) | copy-start | bytes 2949124
  35.6 131.0 %copy-start.3 = (bf16[768,640]{1,0:T(8,128)(2,1)S(1)}, bf16[768,640]{1,0:T(8,128)(2,1)}, u32[]{:S(2)}) copy-start(bf16[768,640]{1,0:T(8,128)(2,1)} %param.6) | copy-start | bytes 2949124
  35.6 124.3 %all-to-all-start.2 = ((bf16[64,1,64,640]{3,2,1,0:T(8,128)(2,1)}), bf16[64,1,64,640]{3,2,1,0:T(8,128)(2,1)}, u32[]{:S(2)}, u32[]{:S(2)}) async-start(bf16[64,1,64,640]{3,2,1,0:T(8,128)(2,1)} %bitcast.41), calls=%async_computation.2 | async-start | bytes 10485760 | tf_op jit(solution)/shard_map/all_to_all | solution.py:45
  159.9 124.4 %all-to-all-start.1 = ((bf16[64,1,64,640]{3,2,1,0:T(8,128)(2,1)}), bf16[64,1,64,640]{3,2,1,0:T(8,128)(2,1)}, u32[]{:S(2)}, u32[]{:S(2)}) async-start(bf16[64,1,64,640]{3,2,1,0:T(8,128)(2,1)} %bitcast.40), calls=%async_computation.1 | async-start | bytes 10485760 | tf_op jit(solution)/shard_map/all_to_all | solution.py:46
  165.9 314.3 %reduce-scatter.2.cloned.1.call-start = ((), (), s32[]{:S(2)}) async-start(), calls=%async_computation.4 | async-start | bytes 19660800 | tf_op jit(solution)/shard_map/reduce_scatter | solution.py:64
  328.9 154.9 %copy-start.1 = (bf16[768,640]{1,0:T(8,128)(2,1)S(1)}, bf16[768,640]{1,0:T(8,128)(2,1)}, u32[]{:S(2)}) copy-start(bf16[768,640]{1,0:T(8,128)(2,1)} %param.7) | copy-start | bytes 2949124
Sparse Core Ops, SparseCore 0:
  341.2 139.0 reduce-scatter.1
where the time goes:
time: 492 us; the launch traced here: 491 us
  waiting for transfers between devices  309 us (63%)
  local copies, waits for them, and re-layouts  64.3 us (13%)
  matrix products  45 us (9%)
  other arithmetic  24.3 us (5%)
  blocking collectives  22.2 us (5%)
  between operations  13.5 us (3%)
  starting transfers between devices  12.1 us (2%)
    reduce_scatter x1, waiting for transfers between devices, per_device(): lax.psum_scatter(partial_out, 'head', scatter_dimension=1, tiled=True)  139 us
    all_to_all x1, waiting for transfers between devices, per_device(): lax.all_to_all(outgoing_keys, 'seq', split_axis=0, concat_axis=0, tiled=T...  115 us
    all_to_all x1, waiting for transfers between devices, per_device(): lax.all_to_all(outgoing_values, 'seq', split_axis=0, concat_axis=0, tiled...  55 us
    all_to_all x1, blocking collectives, per_device(): lax.all_to_all(wanted, 'seq', split_axis=0, concat_axis=0, tiled=True)  22.2 us
    sub x1, other arithmetic, per_device(): raised = jnp.exp(scores - peak)  17.6 us
    dot_general x1, matrix products, per_device(): jnp.einsum('bqhd,bkhd->bhqk', query_blocks, chosen_keys, preferred_elemen...  16.5 us
    dot_general x1, matrix products, per_device(): jnp.einsum('bhqk,bkhd->bqhd', probs, chosen_values, preferred_element_typ...  16.5 us
    gather x1, local copies, waits for them, and re-layouts, per_device(): flat_values[positions].reshape(cubes_here, SEL * CUBE, heads_here, HEAD_DIM)  14.8 us
  transfers between devices with their start and end apart: 3, of which 3 were waited for; matrix products, arithmetic and copies ran while one was open for 14% of the time, Pallas kernels for 0%

commit v1 on v0

v1 whole, which is shorter than its diff:
```python
import functools

import jax
import jax.numpy as jnp
from jax import lax
from jax.experimental import pallas as pl
from jax.experimental.pallas import tpu as pltpu
from jax.sharding import Mesh
from jax.sharding import PartitionSpec as P

HEAD_DIM = 128
CUBE = 64
SEL = 16
NY, NZ, NC = 4, 8, 2
NPLANE = NY * NC


def shift(n, d):
    return [(i, (i + d) % n) for i in range(n)]


def rows_of(at):
    return pl.ds(pl.multiple_of(at * CUBE, CUBE), CUBE)


def pick_kernel(want_ref, from_z_ref, *refs):
    sources, out = refs[:-1], refs[-1]
    width = 2 * HEAD_DIM
    for head, source in enumerate(sources):
        lanes = pl.ds(head * width, width)

        def step(at, carry, source=source, lanes=lanes):
            owner = at % NZ
            out[rows_of(at), lanes] = source[rows_of(from_z_ref[owner] + want_ref[at]), :]
            return carry

        lax.fori_loop(0, NPLANE * NZ, step, 0, unroll=8)


def pick(want, from_z, gathered, first, heads):
    width = 2 * HEAD_DIM
    rows = gathered.shape[0]
    out = jax.ShapeDtypeStruct((NPLANE * NZ * CUBE, heads * width), jnp.bfloat16)
    return pl.pallas_call(
        pick_kernel,
        out_shape=out,
        grid_spec=pltpu.PrefetchScalarGridSpec(
            num_scalar_prefetch=2,
            grid=(1,),
            in_specs=[
                pl.BlockSpec((rows, width), lambda i, *_, at=at: (0, at))
                for at in range(first, first + heads)
            ],
            out_specs=pl.BlockSpec(out.shape, lambda i, *_: (0, 0)),
        ),
        cost_estimate=pl.CostEstimate(flops=0, bytes_accessed=4 * out.size, transcendentals=0),
        compiler_params=pltpu.CompilerParams(vmem_limit_bytes=40 << 20),
        name="pick",
    )(want, from_z, *[gathered] * heads)


def attend_kernel(place_ref, q_ref, *refs, cubes, per):
    arrived, (o_ref, ks, vs) = refs[:-3], refs[-3:]
    for head, kv_ref in enumerate(arrived):
        lanes = pl.ds(head * HEAD_DIM, HEAD_DIM)

        def step(group, carry, kv_ref=kv_ref, lanes=lanes):
            for u in range(per):
                for t in range(SEL):
                    rows = rows_of(place_ref[(group * per + u) * SEL + t])
                    ks[u, t * CUBE : (t + 1) * CUBE, :] = kv_ref[rows, :HEAD_DIM]
                    vs[u, t * CUBE : (t + 1) * CUBE, :] = kv_ref[rows, HEAD_DIM:]
            for u in range(per):
                rows = rows_of(group * per + u)
                scores = lax.dot_general(
                    q_ref[rows, lanes],
                    ks[u],
                    (((1,), (1,)), ((), ())),
                    preferred_element_type=jnp.float32,
                ) * (HEAD_DIM**-0.5)
                peak = jnp.max(scores, axis=1, keepdims=True)
                raised = jnp.exp(scores - peak)
                total = jnp.sum(raised, axis=1, keepdims=True)
                probs = (raised * (1.0 / total)).astype(jnp.bfloat16)
                mixed = jnp.dot(probs, vs[u], preferred_element_type=jnp.float32)
                o_ref[rows, lanes] = mixed.astype(jnp.bfloat16)
            return carry

        lax.fori_loop(0, cubes // per, step, 0)


def attend(places, queries, arrived, first):
    tokens, width = queries.shape[0], len(arrived) * HEAD_DIM
    cubes = tokens // CUBE
    per = next(p for p in (4, 3, 2, 1) if cubes % p == 0)
    return pl.pallas_call(
        functools.partial(attend_kernel, cubes=cubes, per=per),
        out_shape=jax.ShapeDtypeStruct((tokens, width), jnp.bfloat16),
        grid_spec=pltpu.PrefetchScalarGridSpec(
            num_scalar_prefetch=1,
            grid=(1,),
            in_specs=[pl.BlockSpec((tokens, width), lambda i, _: (0, first // len(arrived)))]
            + [
                pl.BlockSpec((a.shape[0], 2 * HEAD_DIM), lambda i, _, at=at: (0, at))
                for a, at in arrived
            ],
            out_specs=pl.BlockSpec((tokens, width), lambda i, _: (0, 0)),
            scratch_shapes=[pltpu.VMEM((per, SEL * CUBE, HEAD_DIM), jnp.bfloat16)] * 2,
        ),
        cost_estimate=pl.CostEstimate(
            flops=4 * tokens * SEL * CUBE * width,
            bytes_accessed=4 * NPLANE * NZ * CUBE * width,
            transcendentals=tokens * SEL * CUBE * len(arrived),
        ),
        compiler_params=pltpu.CompilerParams(vmem_limit_bytes=24 << 20),
        name="attend",
    )(places, queries, *(a for a, _ in arrived))


def project_kernel(*refs, parts, first):
    rows, weights = refs[:parts], refs[parts : 2 * parts]
    total = None if first else refs[2 * parts][...]
    for a, w in zip(rows, weights):
        term = jnp.dot(a[...], w[...], preferred_element_type=jnp.float32)
        total = term if total is None else total + term
    refs[-1][...] = total.astype(refs[-1].dtype)


def project(terms, weights, before, out_type):
    rows = [a for group, _ in terms for a in group]
    parts = len(rows)
    tokens, columns = rows[0].shape[0], weights[0].shape[1]
    tile = 256
    in_specs = [pl.BlockSpec(a.shape, lambda n: (0, 0)) for a in rows]
    in_specs += [
        pl.BlockSpec((a.shape[1], tile), lambda n, at=head * HEAD_DIM // a.shape[1]: (at, n))
        for group, head in terms
        for a in group
    ]
    block = pl.BlockSpec((tokens, tile), lambda n: (0, n))
    extra = [] if before is None else [before]
    return pl.pallas_call(
        functools.partial(project_kernel, parts=parts, first=before is None),
        out_shape=jax.ShapeDtypeStruct((tokens, columns), out_type),
        grid=(columns // tile,),
        in_specs=in_specs + [block] * len(extra),
        out_specs=block,
        cost_estimate=pl.CostEstimate(
            flops=2 * sum(a.size for a in rows) * columns,
            bytes_accessed=8 * tokens * columns,
            transcendentals=0,
        ),
        compiler_params=pltpu.CompilerParams(vmem_limit_bytes=24 << 20),
        name="project",
    )(*rows, *weights * len(terms), *extra)


def after(arrays, earlier):
    held = lax.optimization_barrier(tuple(arrays) + tuple(earlier))
    return held[: len(arrays)]


def per_device(queries, keys, values, w_out, selected, home):
    tokens, width = queries.shape
    cubes_here = tokens // CUBE
    heads_here = width // HEAD_DIM
    groups = lax.axis_size("head")
    y, z, core = (lax.axis_index(a) for a in ("y", "z", "core"))
    me = lax.axis_index("head")

    def columns(a, h):
        return a[:, h * HEAD_DIM : (h + 1) * HEAD_DIM]

    def pack(heads):
        pieces = [columns(a, h) for h in heads for a in (keys, values)]
        return jnp.concatenate(pieces, axis=1)

    catalog = jnp.arange(home.shape[0], dtype=jnp.int32)
    slot_of = jnp.sum(
        jnp.where(selected[:, :, None] == catalog[None, None, :], home[None, None, :], 0), axis=2
    ).reshape(-1)
    owner = slot_of // cubes_here
    places = (owner // (NZ * NC) * NC + owner % NC) * NZ + (z - owner // NC % NZ) % NZ

    every_slot = lax.all_gather(slot_of, ("y", "core"), axis=0)
    owners = every_slot // cubes_here
    mine = (owners // (NZ * NC) == y) & (owners % NC == core)
    step = (z - owners // NC % NZ) % NZ
    matches = mine[:, None, :] & (step[:, None, :] == jnp.arange(NZ, dtype=jnp.int32)[:, None])
    want = jnp.max(jnp.where(matches, every_slot[:, None, :] % cubes_here, 0), axis=2)
    want = want.reshape(-1)
    from_z = (z - jnp.arange(NZ, dtype=jnp.int32)) % NZ * cubes_here

    w_columns = width_out = w_out.shape[1] // groups
    weights = []
    for d in range(groups):
        part = lax.dynamic_slice_in_dim(w_out, (me + d) % groups * w_columns, width_out, axis=1)
        weights.append(lax.ppermute(part, "head", shift(groups, d)) if d else part)

    def exchange(outgoing):
        return lax.all_to_all(outgoing, ("y", "core"), split_axis=0, concat_axis=0, tiled=True)

    def spread(rows):
        return [rows] + [lax.ppermute(rows, "head", shift(groups, d)) for d in range(1, groups)]

    def gather(heads, earlier=()):
        (chunk,) = after((pack(heads),), earlier)
        return lax.all_gather(chunk, "z", axis=0).reshape(NZ * tokens, -1)

    g01 = gather((0, 1))
    g23 = gather((2, 3))
    g4 = gather((4,), (g01,))

    g01, want, _, _ = after((g01, want, weights[1], weights[3]), ())
    in01 = exchange(pick(want, from_z, g01, 0, 2))
    in01, _ = after((in01, weights[2]), ())
    rows01 = attend(places, queries, [(in01, 0), (in01, 1)], 0)

    g23, rows01 = after((g23, rows01), ())
    out2, out3 = pick(want, from_z, g23, 0, 1), pick(want, from_z, g23, 1, 1)
    in2 = exchange(out2)
    rows01, out3 = after((rows01, out3), (out2,))
    all01 = after(spread(rows01), ())

    in2, g4, out3 = after((in2, g4, out3), all01[1:])
    in3 = exchange(out3)
    out4 = pick(want, from_z, g4, 0, 1)
    total = project([(after(all01, (out3,)), 0)], weights, None, jnp.float32)
    rows2 = attend(places, queries, [(in2, 0)], 2)

    in3, out4, rows2 = after((in3, out4, rows2), (total,))
    in4 = exchange(out4)
    rows3 = attend(places, queries, [(in3, 0)], 3)
    all2, all3 = spread(rows2), spread(rows3)
    (in4,) = after((in4,), (rows3,))
    rows4 = attend(places, queries, [(in4, 0)], 4)
    terms = [(all2, 2), (all3, 3), (spread(rows4), 4)]
    return project(terms, weights, total, jnp.bfloat16)


def solution(mesh):
    fine = Mesh(
        mesh.devices.reshape(NY, NZ, NC, mesh.shape["head"]), ("y", "z", "core", "head")
    )
    seq = ("y", "z", "core")
    in_specs = (
        P(seq, "head"),
        P(seq, "head"),
        P(seq, "head"),
        P("head", None),
        P(seq, None),
        P(),
    )
    return jax.shard_map(
        per_device, mesh=fine, in_specs=in_specs, out_specs=P(seq, "head"), check_vma=False
    )
```

time: 492 us -> 316 us (0.64)
  waiting for transfers between devices: 309 us -> 147 us
  Pallas kernels: 0 us -> 58.6 us
  matrix products: 45 us -> 0 us
  starting transfers between devices: 12.1 us -> 44.3 us
  local copies, waits for them, and re-layouts: 64.3 us -> 34.1 us
  other arithmetic: 24.3 us -> 4.41 us
  blocking collectives: 22.2 us -> 12 us
    all_to_all x2 -> x4, waiting for transfers between devices: 170 us -> 25.4 us  [exchange(): lax.all_to_all(outgoing, ('y', 'core'), split_axis=0, concat_axis=0, tile...]
    reduce_scatter x1 -> x0, waiting for transfers between devices: 139 us -> none  [per_device(): lax.psum_scatter(partial_out, 'head', scatter_dimension=1, tiled=True)]
    ppermute x0 -> x15, waiting for transfers between devices: none -> 83.1 us  [the longest x3 58.3 us: per_device(): weights.append(lax.ppermute(part, 'head', shift(groups, d)) if d else part)]
    pallas_call x0 -> x10, Pallas kernels: none -> 58.6 us  [the longest x4 38.9 us: attend(): pl.pallas_call(functools.partial(attend_kernel, cubes=cubes, per=per), ou...]
    dot_general x3 -> x0, matrix products: 45 us -> none  [the longest x1 16.5 us: per_device(): jnp.einsum('bqhd,bkhd->bhqk', query_blocks, chosen_keys, preferred_elemen...]
    all_gather x0 -> x3, waiting for transfers between devices: none -> 38.1 us  [gather(): return lax.all_gather(chunk, 'z', axis=0).reshape(NZ * tokens, -1)]
    gather x4 -> x0, local copies, waits for them, and re-layouts: 36.5 us -> none  [the longest x1 14.8 us: per_device(): flat_values[positions].reshape(cubes_here, SEL * CUBE, heads_here, HEAD_DIM)]
    reshape x4 -> x1, local copies, waits for them, and re-layouts: 26.5 us -> 0.08 us  [per_device(): want = want.reshape(-1)]
  transfers between devices with their start and end apart: 3 -> 22, of which waited for: 3 -> 14; matrix products, arithmetic and copies ran while one was open for 14% -> 3% of each run, Pallas kernels for 0% -> 16%
where the time goes in v1:
time: 316 us; the launch traced here: 313 us
  waiting for transfers between devices  147 us (47%)
  Pallas kernels  58.6 us (19%)
  starting transfers between devices  44.3 us (14%)
  local copies, waits for them, and re-layouts  34.1 us (11%)
  between operations  13.4 us (4%)
  blocking collectives  12 us (4%)
  other arithmetic  4.41 us (1%)
    ppermute x3, waiting for transfers between devices, per_device(): weights.append(lax.ppermute(part, 'head', shift(groups, d)) if d else part)  58.3 us
    pallas_call x4, Pallas kernels, attend(): pl.pallas_call(functools.partial(attend_kernel, cubes=cubes, per=per), ou...  38.9 us
    all_gather x3, waiting for transfers between devices, gather(): return lax.all_gather(chunk, 'z', axis=0).reshape(NZ * tokens, -1)  38.1 us
    unnamed x51, local copies, waits for them, and re-layouts  26 us
    all_to_all x4, waiting for transfers between devices, exchange(): lax.all_to_all(outgoing, ('y', 'core'), split_axis=0, concat_axis=0, tile...  25.4 us
    ppermute x12, waiting for transfers between devices, spread(): lax.ppermute(rows, 'head', shift(groups, d))  24.7 us
    all_to_all x4, starting transfers between devices, exchange(): lax.all_to_all(outgoing, ('y', 'core'), split_axis=0, concat_axis=0, tile...  20.7 us
    ppermute x12, starting transfers between devices, spread(): lax.ppermute(rows, 'head', shift(groups, d))  17.5 us
  transfers between devices with their start and end apart: 22, of which 14 were waited for; matrix products, arithmetic and copies ran while one was open for 3% of the time, Pallas kernels for 16%

profile of v1, /device:TPU:1, one launch (start us, length us, event | category | flops | bytes accessed | tf_op | source)
XLA Modules:
  0.0 313.4 jit_solution(12084044536280458201)
XLA Ops:
  6.5 2.5 fusion.21
  9.0 1.0 pad_maximum_fusion
  10.0 1.0 pad_maximum_fusion.1
  11.1 5.4 %constant_dynamic-slice_fusion.3 = (bf16[640,1280]{1,0:T(8,128)(2,1)S(1)}, bf16[640,1280]{1,0:T(8,128)(2,1)}, bf16[640,1280]{1,0:T(8,128)(2,1)}, bf16[640,1280]{1,0:T(8,128)(2,1)}) fusion(bf16[640,5120]{1,0:T(8,128)(2,1)} %param.9, s32[]{:T(128)S(6)} %select_n.125, s32[]{:T(128)S(6)} %select_n.114, s32[]{:T(128)S(6)} %select_n.112, s32[]{:T(128)S(6)} %select_n.123), kind=kLoop, calls=%fused_computation.71 | loop fusion | bytes 13107216 | tf_op jit(solution)/shard_map/dynamic_slice | solution.py:197
  16.5 2.0 collective-permute-start
  18.5 1.3 collective-permute-start.1
  19.8 0.4 select_reduce_fusion
  20.3 12.0 %all-gather.3 = s32[8,1,192]{2,1,0:T(1,128)S(1)} all-gather(s32[1,1,192]{2,1,0:T(1,128)S(1)} %reshape.52), channel_id=1, replica_groups=mesh['y'=4,'z'=8,'core'=2,'head'=4] {'y','core'}, dimensions={0}, use_global_device_ids=true | all-gather | bytes 6912 | tf_op jit(solution)/shard_map/all_gather | solution.py:185
  32.7 20.6 %collective-permute-done.refs_5_.refs_13_.refs_17_.refs_21_ = bf16[640,1280]{1,0:T(8,128)(2,1)S(1)} collective-permute-done((bf16[640,1280]{1,0:T(8,128)(2,1)}, bf16[640,1280]{1,0:T(8,128)(2,1)S(1)}, u32[]{:S(2)}, u32[]{:S(2)}) %collective-permute-start) | collective-permute-done | bytes 1638432 | tf_op jit(solution)/shard_map/ppermute | solution.py:198
  53.3 1.6 collective-permute-done.1.refs_7_.refs_15_.refs_19_.refs_23_
  54.9 33.5 %all-gather.8.cloned.1.call-done.refs_0_.refs_1_ = bf16[6144,512]{1,0:T(8,128)(2,1)} async-done(((bf16[768,512]{1,0:T(8,128)(2,1)}), bf16[6144,512]{1,0:T(8,128)(2,1)}) %all-gather.8.cloned.1.call-update) | async-done | bytes 6291472 | tf_op jit(solution)/shard_map/all_gather | solution.py:208
  88.4 2.8 copy-done.2
  91.2 1.9 pick.4
  93.1 2.0 copy-done.3
  95.1 5.1 %all-to-all-start = ((bf16[8,512,512]{2,1,0:T(8,128)(2,1)}), bf16[8,512,512]{2,1,0:T(8,128)(2,1)}, u32[]{:S(2)}, u32[]{:S(2)}) async-start(bf16[8,512,512]{2,1,0:T(8,128)(2,1)} %bitcast.40), calls=%async_computation | async-start | bytes 8388608 | tf_op jit(solution)/shard_map/all_to_all | solution.py:201
  100.2 1.7 pad_maximum_fusion.2
  102.0 2.8 collective-permute-start.2
  105.0 36.1 %collective-permute-done.2.refs_6_.refs_14_.refs_18_.refs_22_ = bf16[640,1280]{1,0:T(8,128)(2,1)} collective-permute-done((bf16[640,1280]{1,0:T(8,128)(2,1)}, bf16[640,1280]{1,0:T(8,128)(2,1)}, u32[]{:S(2)}, u32[]{:S(2)}) %collective-permute-start.2) | collective-permute-done | bytes 1638432 | tf_op jit(solution)/shard_map/ppermute | solution.py:198
  141.1 8.0 %all-to-all-done = bf16[8,512,512]{2,1,0:T(8,128)(2,1)} async-done(((bf16[8,512,512]{2,1,0:T(8,128)(2,1)}), bf16[8,512,512]{2,1,0:T(8,128)(2,1)}, u32[]{:S(2)}, u32[]{:S(2)}) %all-to-all-start) | async-done | bytes 4194336 | tf_op jit(solution)/shard_map/all_to_all | solution.py:201
  149.2 1.2 copy-done.6
  150.4 14.1 %attend.4.refs_0_ = bf16[768,256]{1,0:T(8,128)(2,1)S(1)} custom-call(s32[192]{0:T(256)S(1)} %fusion.14.place_ref, bf16[768,640]{1,0:T(8,128)(2,1)S(1)} %copy-done.6, bf16[4096,512]{1,0:T(8,128)(2,1)} %bitcast.3.refs_0_.refs_1_, bf16[4096,512]{1,0:T(8,128)(2,1)} %bitcast.3.refs_0_.refs_1_), custom_call_target="tpu_custom_call" | custom-call | flops 805306368 | bytes 4194304 | tf_op jit(solution)/shard_map/attend/pallas_call | solution.py:96
  164.5 0.7 copy-done.14
  165.3 2.8 copy-done
  168.1 1.2 pick.5
  169.3 1.4 copy-done.11
  170.6 5.1 %all-to-all-start.1 = ((bf16[8,512,256]{2,1,0:T(8,128)(2,1)}), bf16[8,512,256]{2,1,0:T(8,128)(2,1)}, u32[]{:S(2)}, u32[]{:S(2)}) async-start(bf16[8,512,256]{2,1,0:T(8,128)(2,1)} %bitcast.42), calls=%async_computation.1 | async-start | bytes 4194304 | tf_op jit(solution)/shard_map/all_to_all | solution.py:201
  175.7 2.8 copy-done.1
  178.5 1.2 pick.6
  179.7 1.4 copy-done.10
  181.1 1.2 collective-permute-start.3
  182.3 2.4 collective-permute-start.4
  184.7 1.2 collective-permute-start.5
  185.9 7.1 %collective-permute-done.3.refs_1_ = bf16[768,256]{1,0:T(8,128)(2,1)S(1)} collective-permute-done((bf16[768,256]{1,0:T(8,128)(2,1)S(1)}, bf16[768,256]{1,0:T(8,128)(2,1)S(1)}, u32[]{:S(2)}, u32[]{:S(2)}) %collective-permute-start.3) | collective-permute-done | bytes 393248 | tf_op jit(solution)/shard_map/ppermute | solution.py:204
  193.0 0.8 copy-done.17
  193.8 8.6 %collective-permute-done.4.refs_2_ = bf16[768,256]{1,0:T(8,128)(2,1)S(1)} collective-permute-done((bf16[768,256]{1,0:T(8,128)(2,1)S(1)}, bf16[768,256]{1,0:T(8,128)(2,1)S(1)}, u32[]{:S(2)}, u32[]{:S(2)}) %collective-permute-start.4) | collective-permute-done | bytes 393248 | tf_op jit(solution)/shard_map/ppermute | solution.py:204
  202.4 0.7 copy-done.19
  203.1 0.8 copy-done.21
  203.9 4.7 %all-gather.12.cloned.1.call-done.refs_0_ = bf16[6144,256]{1,0:T(8,128)(2,1)} async-done(((bf16[768,256]{1,0:T(8,128)(2,1)}), bf16[6144,256]{1,0:T(8,128)(2,1)}) %all-gather.12.cloned.1.call-update) | async-done | bytes 3145744 | tf_op jit(solution)/shard_map/all_gather | solution.py:208
  208.5 5.2 %all-to-all-start.2 = ((bf16[8,512,256]{2,1,0:T(8,128)(2,1)}), bf16[8,512,256]{2,1,0:T(8,128)(2,1)}, u32[]{:S(2)}, u32[]{:S(2)}) async-start(bf16[8,512,256]{2,1,0:T(8,128)(2,1)} %bitcast.41), calls=%async_computation.2 | async-start | bytes 4194304 | tf_op jit(solution)/shard_map/all_to_all | solution.py:201
  213.7 1.9 copy-done.13
  215.6 1.0 pick.7
  216.8 8.4 %attend.5.refs_0_ = bf16[768,128]{1,0:T(8,128)(2,1)S(1)} custom-call(s32[192]{0:T(256)S(1)} %fusion.14.place_ref, bf16[768,640]{1,0:T(8,128)(2,1)S(1)} %copy-done.7, bf16[4096,256]{1,0:T(8,128)(2,1)} %bitcast.5.refs_0_), custom_call_target="tpu_custom_call" | custom-call | flops 402653184 | bytes 2097152 | tf_op jit(solution)/shard_map/attend/pallas_call | solution.py:96
  225.3 4.9 %project.2.refs_24_ = f32[768,1280]{1,0:T(8,128)S(1)} custom-call(bf16[768,256]{1,0:T(8,128)(2,1)S(1)} %copy-done.16, bf16[768,256]{1,0:T(8,128)(2,1)S(1)} %copy-done.18, bf16[768,256]{1,0:T(8,128)(2,1)S(1)} %copy-done.20, bf16[768,256]{1,0:T(8,128)(2,1)S(1)} %copy-done.22, bf16[640,1280]{1,0:T(8,128)(2,1)S(1)} %get-tuple-element.51.refs_4_.refs_12_.refs_16_.refs_20_, ...), custom_call_target="tpu_custom_call" | custom-call | flops 2013265920 | bytes 7864320 | tf_op jit(solution)/shard_map/project/pallas_call | solution.py:142
  230.2 1.9 copy-done.4
  232.1 8.0 %all-to-all-done.2 = bf16[8,512,256]{2,1,0:T(8,128)(2,1)} async-done(((bf16[8,512,256]{2,1,0:T(8,128)(2,1)}), bf16[8,512,256]{2,1,0:T(8,128)(2,1)}, u32[]{:S(2)}, u32[]{:S(2)}) %all-to-all-start.2) | async-done | bytes 2097184 | tf_op jit(solution)/shard_map/all_to_all | solution.py:201
  240.2 5.3 %all-to-all-start.3 = ((bf16[8,512,256]{2,1,0:T(8,128)(2,1)}), bf16[8,512,256]{2,1,0:T(8,128)(2,1)}, u32[]{:S(2)}, u32[]{:S(2)}) async-start(bf16[8,512,256]{2,1,0:T(8,128)(2,1)} %bitcast.43), calls=%async_computation.3 | async-start | bytes 4194304 | tf_op jit(solution)/shard_map/all_to_all | solution.py:201
  245.4 1.2 copy-done.8
  246.6 8.5 %attend.6.refs_4_ = bf16[768,128]{1,0:T(8,128)(2,1)} custom-call(s32[192]{0:T(256)S(1)} %fusion.14.place_ref, bf16[768,640]{1,0:T(8,128)(2,1)S(1)} %copy-done.8, bf16[4096,256]{1,0:T(8,128)(2,1)} %bitcast.7.refs_0_), custom_call_target="tpu_custom_call" | custom-call | flops 402653184 | bytes 2097152 | tf_op jit(solution)/shard_map/attend/pallas_call | solution.py:96
  255.1 2.7 collective-permute-start.10
  257.8 0.9 collective-permute-start.11
  258.7 0.6 collective-permute-start.9
  259.6 3.0 collective-permute-start.7
  262.6 9.3 %all-to-all-done.3 = bf16[8,512,256]{2,1,0:T(8,128)(2,1)} async-done(((bf16[8,512,256]{2,1,0:T(8,128)(2,1)}), bf16[8,512,256]{2,1,0:T(8,128)(2,1)}, u32[]{:S(2)}, u32[]{:S(2)}) %all-to-all-start.3) | async-done | bytes 2097184 | tf_op jit(solution)/shard_map/all_to_all | solution.py:201
  271.9 1.2 copy-done.9
  273.1 7.8 %attend.7.refs_8_ = bf16[768,128]{1,0:T(8,128)(2,1)S(1)} custom-call(s32[192]{0:T(256)S(1)} %fusion.14.place_ref, bf16[768,640]{1,0:T(8,128)(2,1)S(1)} %copy-done.9, bf16[4096,256]{1,0:T(8,128)(2,1)} %bitcast.9.refs_0_), custom_call_target="tpu_custom_call" | custom-call | flops 402653184 | bytes 2097152 | tf_op jit(solution)/shard_map/attend/pallas_call | solution.py:96
  280.9 2.5 collective-permute-start.8
  283.4 1.7 collective-permute-start.13
  285.2 1.0 collective-permute-start.14
  286.2 0.6 collective-permute-done.8.refs_3_
  286.8 4.0 %collective-permute-done.12.refs_9_ = bf16[768,128]{1,0:T(8,128)(2,1)S(1)} collective-permute-done((bf16[768,128]{1,0:T(8,128)(2,1)S(1)}, bf16[768,128]{1,0:T(8,128)(2,1)S(1)}, u32[]{:S(2)}, u32[]{:S(2)}) %collective-permute-start.12) | collective-permute-done | bytes 196640 | tf_op jit(solution)/shard_map/ppermute | solution.py:204
  290.8 2.4 collective-permute-done.13.refs_10_
  293.2 2.0 collective-permute-done.14.refs_11_
  295.2 2.1 copy-done.5
  297.3 9.6 %project.3 = bf16[768,1280]{1,0:T(8,128)(2,1)} custom-call(bf16[768,128]{1,0:T(8,128)(2,1)S(1)} %attend.5.refs_0_, bf16[768,128]{1,0:T(8,128)(2,1)} %collective-permute-done.6.refs_1_, bf16[768,128]{1,0:T(8,128)(2,1)} %collective-permute-done.7.refs_2_, bf16[768,128]{1,0:T(8,128)(2,1)S(1)} %collective-permute-done.8.refs_3_, ...), custom_call_target="tpu_custom_call" | custom-call | flops 3019898880 | bytes 7864320 | tf_op jit(solution)/shard_map/project/pallas_call | solution.py:142
  (62 shorter events, 1.4 us)
Async XLA Ops:
  6.5 81.9 %all-gather.8.cloned.1.call-start = ((), (), s32[]{:S(2)}) async-start(), calls=%async_computation.4 | async-start | bytes 7077888 | tf_op jit(solution)/shard_map/all_gather | solution.py:208
  10.0 155.3 %all-gather.10.cloned.1.call-start = ((), (), s32[]{:S(2)}) async-start(), calls=%async_computation.5 | async-start | bytes 7077888 | tf_op jit(solution)/shard_map/all_gather | solution.py:208
  11.1 8.7 %copy-start.23 = (s32[12,16]{1,0:T(8,128)S(1)}, s32[12,16]{1,0:T(8,128)}, u32[]{:S(2)}) copy-start(s32[12,16]{1,0:T(8,128)} %param.10) | copy-start | bytes 2308
  11.1 8.7 %copy-start.24 = (s32[768]{0:T(1024)S(1)}, s32[768]{0:T(1024)}, u32[]{:S(2)}) copy-start(s32[768]{0:T(1024)} %param.11) | copy-start | bytes 9220
  16.5 36.8 %collective-permute-start = (bf16[640,1280]{1,0:T(8,128)(2,1)}, bf16[640,1280]{1,0:T(8,128)(2,1)S(1)}, u32[]{:S(2)}, u32[]{:S(2)}) collective-permute-start(bf16[640,1280]{1,0:T(8,128)(2,1)} %get-tuple-element.53), channel_id=1, source_target_pairs={{0,1},{1,2},{2,3},{3,0},{4,5},{5,6},{6,7},{7,4},{8,9},{9,10},{10,1... | collective-permute-start | bytes 4915208 | tf_op jit(solution)/shard_map/ppermute | solution.py:198
  18.5 36.4 %collective-permute-start.1 = (bf16[640,1280]{1,0:T(8,128)(2,1)}, bf16[640,1280]{1,0:T(8,128)(2,1)}, u32[]{:S(2)}, u32[]{:S(2)}) collective-permute-start(bf16[640,1280]{1,0:T(8,128)(2,1)} %get-tuple-element.52), channel_id=1, source_target_pairs={{0,3},{1,0},{2,1},{3,2},{4,7},{5,4},{6,5},{7,6},{8,11},{9,8},{10,9... | collective-permute-start | bytes 4915208 | tf_op jit(solution)/shard_map/ppermute | solution.py:198
  88.4 2.8 copy-start.2
  93.1 2.1 copy-start.3
  95.1 54.0 %all-to-all-start = ((bf16[8,512,512]{2,1,0:T(8,128)(2,1)}), bf16[8,512,512]{2,1,0:T(8,128)(2,1)}, u32[]{:S(2)}, u32[]{:S(2)}) async-start(bf16[8,512,512]{2,1,0:T(8,128)(2,1)} %bitcast.40), calls=%async_computation | async-start | bytes 8388608 | tf_op jit(solution)/shard_map/all_to_all | solution.py:201
  100.2 108.3 %all-gather.12.cloned.1.call-start = ((), (), s32[]{:S(2)}) async-start(), calls=%async_computation.6 | async-start | bytes 3538944 | tf_op jit(solution)/shard_map/all_gather | solution.py:208
  102.0 39.1 %collective-permute-start.2 = (bf16[640,1280]{1,0:T(8,128)(2,1)}, bf16[640,1280]{1,0:T(8,128)(2,1)}, u32[]{:S(2)}, u32[]{:S(2)}) collective-permute-start(bf16[640,1280]{1,0:T(8,128)(2,1)} %get-tuple-element.54), channel_id=1, source_target_pairs={{0,2},{1,3},{2,0},{3,1},{4,6},{5,7},{6,4},{7,5},{8,10},{9,11},{10,... | collective-permute-start | bytes 4915208 | tf_op jit(solution)/shard_map/ppermute | solution.py:198
  149.2 1.2 copy-start.6
  164.5 0.7 copy-start.14
  165.3 2.8 copy-start
  169.3 1.4 copy-start.11
  170.6 33.2 %all-to-all-start.1 = ((bf16[8,512,256]{2,1,0:T(8,128)(2,1)}), bf16[8,512,256]{2,1,0:T(8,128)(2,1)}, u32[]{:S(2)}, u32[]{:S(2)}) async-start(bf16[8,512,256]{2,1,0:T(8,128)(2,1)} %bitcast.42), calls=%async_computation.1 | async-start | bytes 4194304 | tf_op jit(solution)/shard_map/all_to_all | solution.py:201
  175.7 2.8 copy-start.1
  178.5 2.6 copy-start.15
  179.7 1.4 copy-start.10
  181.1 11.9 %collective-permute-start.3 = (bf16[768,256]{1,0:T(8,128)(2,1)S(1)}, bf16[768,256]{1,0:T(8,128)(2,1)S(1)}, u32[]{:S(2)}, u32[]{:S(2)}) collective-permute-start(bf16[768,256]{1,0:T(8,128)(2,1)S(1)} %copy-done.15), channel_id=1, source_target_pairs={{0,1},{1,2},{2,3},{3,0},{4,5},{5,6},{6,7},{7,4},{8,9},{9,10},{10,1... | collective-permute-start | bytes 1179656 | tf_op jit(solution)/shard_map/ppermute | solution.py:204
  182.3 20.0 %collective-permute-start.4 = (bf16[768,256]{1,0:T(8,128)(2,1)S(1)}, bf16[768,256]{1,0:T(8,128)(2,1)S(1)}, u32[]{:S(2)}, u32[]{:S(2)}) collective-permute-start(bf16[768,256]{1,0:T(8,128)(2,1)S(1)} %copy-done.15), channel_id=1, source_target_pairs={{0,2},{1,3},{2,0},{3,1},{4,6},{5,7},{6,4},{7,5},{8,10},{9,11},{10,... | collective-permute-start | bytes 1179656 | tf_op jit(solution)/shard_map/ppermute | solution.py:204
  184.7 18.4 %collective-permute-start.5 = (bf16[768,256]{1,0:T(8,128)(2,1)S(1)}, bf16[768,256]{1,0:T(8,128)(2,1)S(1)}, u32[]{:S(2)}, u32[]{:S(2)}) collective-permute-start(bf16[768,256]{1,0:T(8,128)(2,1)S(1)} %copy-done.15), channel_id=1, source_target_pairs={{0,3},{1,0},{2,1},{3,2},{4,7},{5,4},{6,5},{7,6},{8,11},{9,8},{10,9... | collective-permute-start | bytes 1179656 | tf_op jit(solution)/shard_map/ppermute | solution.py:204
  193.0 0.8 copy-start.17
  202.4 0.7 copy-start.19
  203.1 0.8 copy-start.21
  208.5 31.6 %all-to-all-start.2 = ((bf16[8,512,256]{2,1,0:T(8,128)(2,1)}), bf16[8,512,256]{2,1,0:T(8,128)(2,1)}, u32[]{:S(2)}, u32[]{:S(2)}) async-start(bf16[8,512,256]{2,1,0:T(8,128)(2,1)} %bitcast.41), calls=%async_computation.2 | async-start | bytes 4194304 | tf_op jit(solution)/shard_map/all_to_all | solution.py:201
  213.7 1.9 copy-start.13
  215.6 1.2 copy-start.7
  216.8 8.5 %copy-start.12 = (bf16[4096,256]{1,0:T(8,128)(2,1)}, bf16[4096,256]{1,0:T(8,128)(2,1)S(1)}, u32[]{:S(2)}) copy-start(bf16[4096,256]{1,0:T(8,128)(2,1)S(1)} %pick.7) | copy-start | bytes 6291460
  216.8 8.5 %copy-start.16 = (bf16[768,256]{1,0:T(8,128)(2,1)S(1)}, bf16[768,256]{1,0:T(8,128)(2,1)}, u32[]{:S(2)}) copy-start(bf16[768,256]{1,0:T(8,128)(2,1)} %copy-done.14) | copy-start | bytes 1179652
  216.8 8.5 %copy-start.18 = (bf16[768,256]{1,0:T(8,128)(2,1)S(1)}, bf16[768,256]{1,0:T(8,128)(2,1)}, u32[]{:S(2)}) copy-start(bf16[768,256]{1,0:T(8,128)(2,1)} %copy-done.17) | copy-start | bytes 1179652
  216.8 8.5 %copy-start.20 = (bf16[768,256]{1,0:T(8,128)(2,1)S(1)}, bf16[768,256]{1,0:T(8,128)(2,1)}, u32[]{:S(2)}) copy-start(bf16[768,256]{1,0:T(8,128)(2,1)} %copy-done.19) | copy-start | bytes 1179652
  216.8 8.5 %copy-start.22 = (bf16[768,256]{1,0:T(8,128)(2,1)S(1)}, bf16[768,256]{1,0:T(8,128)(2,1)}, u32[]{:S(2)}) copy-start(bf16[768,256]{1,0:T(8,128)(2,1)} %copy-done.21) | copy-start | bytes 1179652
  230.2 1.9 copy-start.4
  240.2 31.7 %all-to-all-start.3 = ((bf16[8,512,256]{2,1,0:T(8,128)(2,1)}), bf16[8,512,256]{2,1,0:T(8,128)(2,1)}, u32[]{:S(2)}, u32[]{:S(2)}) async-start(bf16[8,512,256]{2,1,0:T(8,128)(2,1)} %bitcast.43), calls=%async_computation.3 | async-start | bytes 4194304 | tf_op jit(solution)/shard_map/all_to_all | solution.py:201
  245.4 1.2 copy-start.8
  255.1 25.8 %collective-permute-start.10 = (bf16[768,128]{1,0:T(8,128)(2,1)}, bf16[768,128]{1,0:T(8,128)(2,1)}, u32[]{:S(2)}, u32[]{:S(2)}) collective-permute-start(bf16[768,128]{1,0:T(8,128)(2,1)} %attend.6.refs_4_), channel_id=1, source_target_pairs={{0,2},{1,3},{2,0},{3,1},{4,6},{5,7},{6,4},{7,5},{8,10},{9,11},{10,... | collective-permute-start | bytes 589832 | tf_op jit(solution)/shard_map/ppermute | solution.py:204
  257.8 25.6 %collective-permute-start.11 = (bf16[768,128]{1,0:T(8,128)(2,1)}, bf16[768,128]{1,0:T(8,128)(2,1)}, u32[]{:S(2)}, u32[]{:S(2)}) collective-permute-start(bf16[768,128]{1,0:T(8,128)(2,1)} %attend.6.refs_4_), channel_id=1, source_target_pairs={{0,3},{1,0},{2,1},{3,2},{4,7},{5,4},{6,5},{7,6},{8,11},{9,8},{10,9... | collective-permute-start | bytes 589832 | tf_op jit(solution)/shard_map/ppermute | solution.py:204
  258.7 24.7 %collective-permute-start.9 = (bf16[768,128]{1,0:T(8,128)(2,1)}, bf16[768,128]{1,0:T(8,128)(2,1)}, u32[]{:S(2)}, u32[]{:S(2)}) collective-permute-start(bf16[768,128]{1,0:T(8,128)(2,1)} %attend.6.refs_4_), channel_id=1, source_target_pairs={{0,1},{1,2},{2,3},{3,0},{4,5},{5,6},{6,7},{7,4},{8,9},{9,10},{10,1... | collective-permute-start | bytes 589832 | tf_op jit(solution)/shard_map/ppermute | solution.py:204
  259.3 25.9 %collective-permute-start.6 = (bf16[768,128]{1,0:T(8,128)(2,1)S(1)}, bf16[768,128]{1,0:T(8,128)(2,1)}, u32[]{:S(2)}, u32[]{:S(2)}) collective-permute-start(bf16[768,128]{1,0:T(8,128)(2,1)S(1)} %attend.5.refs_0_), channel_id=1, source_target_pairs={{0,1},{1,2},{2,3},{3,0},{4,5},{5,6},{6,7},{7,4},{8,9},{9,10},{10,1... | collective-permute-start | bytes 589832 | tf_op jit(solution)/shard_map/ppermute | solution.py:204
  259.6 26.6 %collective-permute-start.7 = (bf16[768,128]{1,0:T(8,128)(2,1)S(1)}, bf16[768,128]{1,0:T(8,128)(2,1)}, u32[]{:S(2)}, u32[]{:S(2)}) collective-permute-start(bf16[768,128]{1,0:T(8,128)(2,1)S(1)} %attend.5.refs_0_), channel_id=1, source_target_pairs={{0,2},{1,3},{2,0},{3,1},{4,6},{5,7},{6,4},{7,5},{8,10},{9,11},{10,... | collective-permute-start | bytes 589832 | tf_op jit(solution)/shard_map/ppermute | solution.py:204
  271.9 1.2 copy-start.9
  280.9 5.8 %collective-permute-start.8 = (bf16[768,128]{1,0:T(8,128)(2,1)S(1)}, bf16[768,128]{1,0:T(8,128)(2,1)S(1)}, u32[]{:S(2)}, u32[]{:S(2)}) collective-permute-start(bf16[768,128]{1,0:T(8,128)(2,1)S(1)} %attend.5.refs_0_), channel_id=1, source_target_pairs={{0,3},{1,0},{2,1},{3,2},{4,7},{5,4},{6,5},{7,6},{8,11},{9,8},{10,9... | collective-permute-start | bytes 589832 | tf_op jit(solution)/shard_map/ppermute | solution.py:204
  283.4 7.4 %collective-permute-start.12 = (bf16[768,128]{1,0:T(8,128)(2,1)S(1)}, bf16[768,128]{1,0:T(8,128)(2,1)S(1)}, u32[]{:S(2)}, u32[]{:S(2)}) collective-permute-start(bf16[768,128]{1,0:T(8,128)(2,1)S(1)} %attend.7.refs_8_), channel_id=1, source_target_pairs={{0,1},{1,2},{2,3},{3,0},{4,5},{5,6},{6,7},{7,4},{8,9},{9,10},{10,1... | collective-permute-start | bytes 589832 | tf_op jit(solution)/shard_map/ppermute | solution.py:204
  283.4 9.7 %collective-permute-start.13 = (bf16[768,128]{1,0:T(8,128)(2,1)S(1)}, bf16[768,128]{1,0:T(8,128)(2,1)S(1)}, u32[]{:S(2)}, u32[]{:S(2)}) collective-permute-start(bf16[768,128]{1,0:T(8,128)(2,1)S(1)} %attend.7.refs_8_), channel_id=1, source_target_pairs={{0,2},{1,3},{2,0},{3,1},{4,6},{5,7},{6,4},{7,5},{8,10},{9,11},{10,... | collective-permute-start | bytes 589832 | tf_op jit(solution)/shard_map/ppermute | solution.py:204
  285.2 10.0 %collective-permute-start.14 = (bf16[768,128]{1,0:T(8,128)(2,1)S(1)}, bf16[768,128]{1,0:T(8,128)(2,1)S(1)}, u32[]{:S(2)}, u32[]{:S(2)}) collective-permute-start(bf16[768,128]{1,0:T(8,128)(2,1)S(1)} %attend.7.refs_8_), channel_id=1, source_target_pairs={{0,3},{1,0},{2,1},{3,2},{4,7},{5,4},{6,5},{7,6},{8,11},{9,8},{10,9... | collective-permute-start | bytes 589832 | tf_op jit(solution)/shard_map/ppermute | solution.py:204
  295.2 2.1 copy-start.5
Sparse Core Ops, SparseCore 0:
  10.1 78.2 all-gather.7
  90.2 73.0 all-gather.9
  165.1 43.3 all-gather.11

commit v2 on v1

v2 whole, which is shorter than its diff:
```python
import functools

import jax
import jax.numpy as jnp
from jax import lax
from jax.experimental import pallas as pl
from jax.experimental.pallas import tpu as pltpu
from jax.sharding import Mesh
from jax.sharding import PartitionSpec as P

HEAD_DIM = 128
CUBE = 64
SEL = 16
NY, NZ, NC = 4, 8, 2
NPLANE = NY * NC
LOG2_E = 1.4426950408889634


def shift(n, d):
    return [(i, (i + d) % n) for i in range(n)]


def rows_of(at):
    return pl.ds(pl.multiple_of(at * CUBE, CUBE), CUBE)


def pick_kernel(cube_ref, *refs, blocks):
    sources, out = refs[:-1], refs[-1]
    width = 2 * HEAD_DIM
    for head, source in enumerate(sources):
        lanes = pl.ds(head * width, width)

        def step(at, carry, source=source, lanes=lanes):
            out[rows_of(at), lanes] = source[rows_of(cube_ref[at]), :]
            return carry

        lax.fori_loop(0, blocks, step, 0, unroll=8)


def pick(cubes, source, first, heads):
    width = 2 * HEAD_DIM
    rows, blocks = source.shape[0], cubes.shape[0]
    out = jax.ShapeDtypeStruct((blocks * CUBE, heads * width), jnp.bfloat16)
    return pl.pallas_call(
        functools.partial(pick_kernel, blocks=blocks),
        out_shape=out,
        grid_spec=pltpu.PrefetchScalarGridSpec(
            num_scalar_prefetch=1,
            grid=(1,),
            in_specs=[
                pl.BlockSpec((rows, width), lambda i, *_, at=at: (0, at))
                for at in range(first, first + heads)
            ],
            out_specs=pl.BlockSpec(out.shape, lambda i, *_: (0, 0)),
        ),
        cost_estimate=pl.CostEstimate(flops=0, bytes_accessed=4 * out.size, transcendentals=0),
        compiler_params=pltpu.CompilerParams(vmem_limit_bytes=40 << 20),
        name="pick",
    )(cubes, *[source] * heads)


def attend_kernel(place_ref, *refs, cubes, per):
    heads = (len(refs) - 3) // 2
    asking, arrived, (o_ref, ks, vs) = refs[:heads], refs[heads:-3], refs[-3:]
    for head in range(heads):
        lanes = pl.ds(head * HEAD_DIM, HEAD_DIM)

        def step(group, carry, q_ref=asking[head], kv_ref=arrived[head], lanes=lanes):
            for u in range(per):
                for t in range(SEL):
                    rows = rows_of(place_ref[(group * per + u) * SEL + t])
                    ks[u, t * CUBE : (t + 1) * CUBE, :] = kv_ref[rows, :HEAD_DIM]
                    vs[u, t * CUBE : (t + 1) * CUBE, :] = kv_ref[rows, HEAD_DIM:]
            for u in range(per):
                rows = rows_of(group * per + u)
                scores = lax.dot_general(
                    q_ref[rows, :],
                    ks[u],
                    (((1,), (1,)), ((), ())),
                    preferred_element_type=jnp.float32,
                )
                peak = jnp.max(scores, axis=1, keepdims=True)
                raised = jnp.exp2((scores - peak) * (HEAD_DIM**-0.5 * LOG2_E))
                total = jnp.sum(raised, axis=1, keepdims=True)
                probs = (raised * (1.0 / total)).astype(jnp.bfloat16)
                mixed = jnp.dot(probs, vs[u], preferred_element_type=jnp.float32)
                o_ref[rows, lanes] = mixed.astype(jnp.bfloat16)
            return carry

        lax.fori_loop(0, cubes // per, step, 0)


def attend(places, queries, arrived, first):
    tokens, width = queries.shape[0], len(arrived) * HEAD_DIM
    cubes = tokens // CUBE
    per = next(p for p in (4, 3, 2, 1) if cubes % p == 0)
    return pl.pallas_call(
        functools.partial(attend_kernel, cubes=cubes, per=per),
        out_shape=jax.ShapeDtypeStruct((tokens, width), jnp.bfloat16),
        grid_spec=pltpu.PrefetchScalarGridSpec(
            num_scalar_prefetch=1,
            grid=(1,),
            in_specs=[
                pl.BlockSpec((tokens, HEAD_DIM), lambda i, _, head=head: (0, head))
                for head in range(first, first + len(arrived))
            ]
            + [
                pl.BlockSpec((a.shape[0], 2 * HEAD_DIM), lambda i, _, at=at: (0, at))
                for a, at in arrived
            ],
            out_specs=pl.BlockSpec((tokens, width), lambda i, _: (0, 0)),
            scratch_shapes=[pltpu.VMEM((per, SEL * CUBE, HEAD_DIM), jnp.bfloat16)] * 2,
        ),
        cost_estimate=pl.CostEstimate(
            flops=4 * tokens * SEL * CUBE * width,
            bytes_accessed=4 * NPLANE * NZ * CUBE * width,
            transcendentals=tokens * SEL * CUBE * len(arrived),
        ),
        compiler_params=pltpu.CompilerParams(vmem_limit_bytes=24 << 20),
        name="attend",
    )(places, *[queries] * len(arrived), *(a for a, _ in arrived))


def project_kernel(*refs, terms, heads):
    rows, weights, before = refs[:terms], refs[terms : terms + heads], refs[terms + heads : -2]
    out, beside = refs[-2:]

    @pl.when(pl.program_id(0) == 0)
    def _():
        at = 0
        for a in rows:
            beside[:, at : at + a.shape[1]] = a[...]
            at += a.shape[1]

    below = jnp.concatenate([w[...] for w in weights], axis=0)
    total = jnp.dot(beside[...], below, preferred_element_type=jnp.float32)
    for earlier in before:
        total = total + earlier[...]
    out[...] = total.astype(out.dtype)


def project(terms, weights, before, out_type):
    rows = [a for group, _ in terms for a in group]
    tokens, columns = rows[0].shape[0], weights[0].shape[1]
    tile = 256
    block = pl.BlockSpec((tokens, tile), lambda n: (0, n))
    in_specs = [pl.BlockSpec(a.shape, lambda n: (0, 0)) for a in rows]
    below = []
    for group, first in terms:
        for a, w in zip(group, weights):
            for head in range(first, first + a.shape[1] // HEAD_DIM):
                in_specs.append(pl.BlockSpec((HEAD_DIM, tile), lambda n, head=head: (head, n)))
                below.append(w)
    extra = [] if before is None else [before]
    width = sum(a.shape[1] for a in rows)
    return pl.pallas_call(
        functools.partial(project_kernel, terms=len(rows), heads=len(below)),
        out_shape=jax.ShapeDtypeStruct((tokens, columns), out_type),
        grid=(columns // tile,),
        in_specs=in_specs + [block] * len(extra),
        out_specs=block,
        scratch_shapes=[pltpu.VMEM((tokens, width), jnp.bfloat16)],
        cost_estimate=pl.CostEstimate(
            flops=2 * tokens * width * columns,
            bytes_accessed=2 * (tokens * width + width * columns + tokens * columns),
            transcendentals=0,
        ),
        compiler_params=pltpu.CompilerParams(vmem_limit_bytes=40 << 20),
        name="project",
    )(*rows, *below, *extra)


def after(arrays, earlier):
    held = lax.optimization_barrier(tuple(arrays) + tuple(earlier))
    return held[: len(arrays)]


def per_device(queries, keys, values, w_out, selected, home):
    tokens, width = queries.shape
    cubes_here = tokens // CUBE
    heads_here = width // HEAD_DIM
    groups = lax.axis_size("head")
    y, z, core = (lax.axis_index(a) for a in ("y", "z", "core"))
    me = lax.axis_index("head")

    def columns(a, h):
        return a[:, h * HEAD_DIM : (h + 1) * HEAD_DIM]

    def exchange(outgoing):
        return lax.all_to_all(outgoing, ("y", "core"), split_axis=0, concat_axis=0, tiled=True)

    def pack(heads):
        pieces = [columns(a, h) for h in heads for a in (keys, values)]
        return jnp.concatenate(pieces, axis=1)

    catalog = jnp.arange(home.shape[0], dtype=jnp.int32)
    slot_of = jnp.sum(
        jnp.where(selected[:, :, None] == catalog[None, None, :], home[None, None, :], 0), axis=2
    ).reshape(-1)
    owner = slot_of // cubes_here
    places = (owner // (NZ * NC) * NC + owner % NC) * NZ + (z - owner // NC % NZ) % NZ

    plane = lax.all_gather(slot_of, ("y", "core"), axis=0)
    owners = plane // cubes_here
    mine = (owners // (NZ * NC) == y) & (owners % NC == core)
    step = (z - owners // NC % NZ) % NZ
    steps = jnp.arange(NZ, dtype=jnp.int32)[:, None]
    matches = mine[:, None, :] & (step[:, None, :] == steps)
    want = jnp.max(jnp.where(matches, plane[:, None, :] % cubes_here, 0), axis=2)
    from_z = (z - steps[:, 0]) % NZ * cubes_here
    want = (want + from_z).reshape(-1)

    w_columns = width_out = w_out.shape[1] // groups
    weights = []
    for d in range(groups):
        part = lax.dynamic_slice_in_dim(w_out, (me + d) % groups * w_columns, width_out, axis=1)
        weights.append(lax.ppermute(part, "head", shift(groups, d)) if d else part)

    def spread(rows):
        return [rows] + [lax.ppermute(rows, "head", shift(groups, d)) for d in range(1, groups)]

    def gather(heads, earlier=()):
        (chunk,) = after((pack(heads),), earlier)
        return lax.all_gather(chunk, "z", axis=0).reshape(NZ * tokens, -1)

    g0 = gather((0,))
    g12 = gather((1, 2))

    g0, want = after((g0, want), ())
    out0 = pick(want, g0, 0, 1)
    in0 = exchange(out0)
    g3 = gather((3,), (out0,))
    rows0 = attend(places, queries, [(in0, 0)], 0)
    all0 = spread(rows0)

    (g12,) = after((g12,), all0[1:] + [weights[1], weights[3]])
    out12 = pick(want, g12, 0, 2)
    in12 = exchange(out12)
    g4 = gather((4,), (out12,))
    out3 = pick(want, g3, 0, 1)
    in12, out3 = after((in12, out3), (weights[2],))
    in3 = exchange(out3)
    rows12 = attend(places, queries, [(in12, 0), (in12, 1)], 1)
    all12 = spread(rows12)

    g4, _ = after((g4, rows12), ())
    out4 = pick(want, g4, 0, 1)
    in3, out4 = after((in3, out4), ())
    in4 = exchange(out4)
    rows3 = attend(places, queries, [(in3, 0)], 3)
    all3 = spread(rows3)

    (in4,) = after((in4,), (rows3,))
    rows4 = attend(places, queries, [(in4, 0)], 4)
    all4 = spread(rows4)
    held = after(all0 + all12 + all3, (rows4,))
    terms = [(held[:groups], 0), (held[groups : 2 * groups], 1), (held[2 * groups :], 3)]
    total = project(terms, weights, None, jnp.float32)
    return project([(all4, 4)], weights, total, jnp.bfloat16)


def solution(mesh):
    fine = Mesh(
        mesh.devices.reshape(NY, NZ, NC, mesh.shape["head"]), ("y", "z", "core", "head")
    )
    seq = ("y", "z", "core")
    in_specs = (
        P(seq, "head"),
        P(seq, "head"),
        P(seq, "head"),
        P("head", None),
        P(seq, None),
        P(),
    )
    return jax.shard_map(
        per_device, mesh=fine, in_specs=in_specs, out_specs=P(seq, "head"), check_vma=False
    )
```

time: 316 us -> 296 us (0.937)
  waiting for transfers between devices: 147 us -> 140 us
  local copies, waits for them, and re-layouts: 34.1 us -> 28.9 us
  starting transfers between devices: 44.3 us -> 40.2 us
    ppermute x3, waiting for transfers between devices: 58.3 us -> 12.6 us  [per_device(): weights.append(lax.ppermute(part, 'head', shift(groups, d)) if d else part)]
    all_gather x3 -> x4, waiting for transfers between devices: 38.1 us -> 83.4 us  [gather(): return lax.all_gather(chunk, 'z', axis=0).reshape(NZ * tokens, -1)]
    ppermute x12, waiting for transfers between devices: 24.7 us -> 9.48 us  [spread(): lax.ppermute(rows, 'head', shift(groups, d))]
    all_to_all x4, waiting for transfers between devices: 25.4 us -> 34.4 us  [exchange(): lax.all_to_all(outgoing, ('y', 'core'), split_axis=0, concat_axis=0, tile...]
    unnamed x51 -> x49, local copies, waits for them, and re-layouts: 26 us -> 21.7 us
    ppermute x12, starting transfers between devices: 17.5 us -> 14.2 us  [spread(): lax.ppermute(rows, 'head', shift(groups, d))]
  transfers between devices with their start and end apart: 22 -> 23, of which waited for: 14 -> 14; matrix products, arithmetic and copies ran while one was open for 3% -> 3% of each run, Pallas kernels for 16% -> 17%
where the time goes in v2:
time: 296 us; the launch traced here: 295 us
  waiting for transfers between devices  140 us (47%)
  Pallas kernels  56.2 us (19%)
  starting transfers between devices  40.2 us (14%)
  local copies, waits for them, and re-layouts  28.9 us (10%)
  between operations  13.5 us (5%)
  blocking collectives  12.1 us (4%)
  other arithmetic  3.5 us (1%)
    all_gather x4, waiting for transfers between devices, gather(): return lax.all_gather(chunk, 'z', axis=0).reshape(NZ * tokens, -1)  83.4 us
    pallas_call x4, Pallas kernels, attend(): pl.pallas_call(functools.partial(attend_kernel, cubes=cubes, per=per), ou...  38.1 us
    all_to_all x4, waiting for transfers between devices, exchange(): lax.all_to_all(outgoing, ('y', 'core'), split_axis=0, concat_axis=0, tile...  34.4 us
    unnamed x49, local copies, waits for them, and re-layouts  21.7 us
    all_to_all x4, starting transfers between devices, exchange(): lax.all_to_all(outgoing, ('y', 'core'), split_axis=0, concat_axis=0, tile...  20.7 us
    ppermute x12, starting transfers between devices, spread(): lax.ppermute(rows, 'head', shift(groups, d))  14.2 us
    pallas_call x2, Pallas kernels, project(): pl.pallas_call(functools.partial(project_kernel, terms=len(rows), heads=l...  12.9 us
    ppermute x3, waiting for transfers between devices, per_device(): weights.append(lax.ppermute(part, 'head', shift(groups, d)) if d else part)  12.6 us
  transfers between devices with their start and end apart: 23, of which 14 were waited for; matrix products, arithmetic and copies ran while one was open for 3% of the time, Pallas kernels for 17%

profile of v2, /device:TPU:1, one launch (start us, length us, event | category | flops | bytes accessed | tf_op | source)
XLA Modules:
  0.0 294.7 jit_solution(9096266595634827895)
XLA Ops:
  6.5 1.4 fusion.21
  8.4 0.8 pad_maximum_fusion.1
  9.2 1.0 pad_maximum_fusion
  10.8 12.1 %all-gather.4 = s32[8,1,192]{2,1,0:T(1,128)S(1)} all-gather(s32[1,1,192]{2,1,0:T(1,128)S(1)} %reshape.74), channel_id=1, replica_groups=mesh['y'=4,'z'=8,'core'=2,'head'=4] {'y','core'}, dimensions={0}, use_global_device_ids=true | all-gather | bytes 6912 | tf_op jit(solution)/shard_map/all_gather | solution.py:203
  23.3 1.0 pad_maximum_fusion.2
  24.3 33.6 %all-gather.10.cloned.1.call-done.refs_0_ = bf16[6144,256]{1,0:T(8,128)(2,1)} async-done(((bf16[768,256]{1,0:T(8,128)(2,1)}), bf16[6144,256]{1,0:T(8,128)(2,1)}) %all-gather.10.cloned.1.call-update) | async-done | bytes 3145744 | tf_op jit(solution)/shard_map/all_gather | solution.py:224
  57.9 1.9 copy-done.9
  59.8 2.2 pick.4
  62.0 5.2 %all-to-all-start = ((bf16[8,512,256]{2,1,0:T(8,128)(2,1)}), bf16[8,512,256]{2,1,0:T(8,128)(2,1)}, u32[]{:S(2)}, u32[]{:S(2)}) async-start(bf16[8,512,256]{2,1,0:T(8,128)(2,1)} %bitcast.2), calls=%async_computation | async-start | bytes 4194304 | tf_op jit(solution)/shard_map/all_to_all | solution.py:190
  67.2 5.3 %constant_dynamic-slice_fusion.3 = (bf16[640,1280]{1,0:T(8,128)(2,1)S(1)}, bf16[640,1280]{1,0:T(8,128)(2,1)}, bf16[640,1280]{1,0:T(8,128)(2,1)}, bf16[640,1280]{1,0:T(8,128)(2,1)}) fusion(bf16[640,5120]{1,0:T(8,128)(2,1)} %param.9, s32[]{:T(128)S(6)} %select_n.129, s32[]{:T(128)S(6)} %select_n.125, s32[]{:T(128)S(6)} %select_n.123, s32[]{:T(128)S(6)} %select_n.127), kind=kLoop, calls=%fused_computation.73 | loop fusion | bytes 13107216 | tf_op jit(solution)/shard_map/dynamic_slice | solution.py:216
  72.5 2.4 collective-permute-start.4
  75.2 18.5 %all-to-all-done = bf16[8,512,256]{2,1,0:T(8,128)(2,1)} async-done(((bf16[8,512,256]{2,1,0:T(8,128)(2,1)}), bf16[8,512,256]{2,1,0:T(8,128)(2,1)}, u32[]{:S(2)}, u32[]{:S(2)}) %all-to-all-start) | async-done | bytes 2097184 | tf_op jit(solution)/shard_map/all_to_all | solution.py:190
  93.7 1.2 copy-done.1
  94.9 7.8 %attend.4.refs_0_ = bf16[768,128]{1,0:T(8,128)(2,1)S(1)} custom-call(s32[192]{0:T(256)S(1)} %fusion.14.place_ref, bf16[768,640]{1,0:T(8,128)(2,1)S(1)} %copy-done.1, bf16[4096,256]{1,0:T(8,128)(2,1)} %bitcast.3.refs_1_), custom_call_target="tpu_custom_call" | custom-call | flops 402653184 | bytes 2097152 | tf_op jit(solution)/shard_map/attend/pallas_call | solution.py:97
  102.7 2.5 collective-permute-start.2
  105.2 0.6 collective-permute-start.1
  105.8 0.6 collective-permute-start
  106.3 4.1 %collective-permute-done.4.refs_15_.refs_22_.refs_23_.refs_27_.refs_7_ = bf16[640,1280]{1,0:T(8,128)(2,1)S(1)} collective-permute-done((bf16[640,1280]{1,0:T(8,128)(2,1)}, bf16[640,1280]{1,0:T(8,128)(2,1)S(1)}, u32[]{:S(2)}, u32[]{:S(2)}) %collective-permute-start.4) | collective-permute-done | bytes 1638432 | tf_op jit(solution)/shard_map/ppermute | solution.py:217
  110.4 6.6 %collective-permute-done.3.refs_13_.refs_18_.refs_19_.refs_25_.refs_5_ = bf16[640,1280]{1,0:T(8,128)(2,1)} collective-permute-done((bf16[640,1280]{1,0:T(8,128)(2,1)}, bf16[640,1280]{1,0:T(8,128)(2,1)}, u32[]{:S(2)}, u32[]{:S(2)}) %collective-permute-start.3) | collective-permute-done | bytes 1638432 | tf_op jit(solution)/shard_map/ppermute | solution.py:217
  117.0 1.6 collective-permute-done.2.refs_3_
  118.6 0.7 copy-done.15
  119.3 0.7 copy-done.17
  119.9 2.0 collective-permute-done.refs_1_
  121.9 0.7 copy-done.19
  122.6 10.4 %all-gather.12.cloned.1.call-done.refs_0_.refs_1_ = bf16[6144,512]{1,0:T(8,128)(2,1)} async-done(((bf16[768,512]{1,0:T(8,128)(2,1)}), bf16[6144,512]{1,0:T(8,128)(2,1)}) %all-gather.12.cloned.1.call-update) | async-done | bytes 6291472 | tf_op jit(solution)/shard_map/all_gather | solution.py:224
  133.0 2.8 copy-done
  135.8 1.5 pick.5
  137.3 2.0 copy-done.5
  139.3 5.1 %all-to-all-start.1 = ((bf16[8,512,512]{2,1,0:T(8,128)(2,1)}), bf16[8,512,512]{2,1,0:T(8,128)(2,1)}, u32[]{:S(2)}, u32[]{:S(2)}) async-start(bf16[8,512,512]{2,1,0:T(8,128)(2,1)} %bitcast.40), calls=%async_computation.1 | async-start | bytes 8388608 | tf_op jit(solution)/shard_map/all_to_all | solution.py:190
  144.4 0.6 all-gather.16.cloned.1.call-update
  145.0 2.8 collective-permute-start.5
  147.8 30.5 %all-gather.14.cloned.1.call-done.refs_0_ = bf16[6144,256]{1,0:T(8,128)(2,1)} async-done(((bf16[768,256]{1,0:T(8,128)(2,1)}), bf16[6144,256]{1,0:T(8,128)(2,1)}) %all-gather.14.cloned.1.call-update) | async-done | bytes 3145744 | tf_op jit(solution)/shard_map/all_gather | solution.py:224
  178.2 1.9 copy-done.8
  180.1 0.8 pick.6
  180.9 1.3 copy-done.7
  182.2 1.9 collective-permute-done.5.refs_14_.refs_20_.refs_21_.refs_26_.refs_6_
  184.1 9.2 %all-to-all-done.1 = bf16[8,512,512]{2,1,0:T(8,128)(2,1)} async-done(((bf16[8,512,512]{2,1,0:T(8,128)(2,1)}), bf16[8,512,512]{2,1,0:T(8,128)(2,1)}, u32[]{:S(2)}, u32[]{:S(2)}) %all-to-all-start.1) | async-done | bytes 4194336 | tf_op jit(solution)/shard_map/all_to_all | solution.py:190
  193.3 5.1 %all-to-all-start.2 = ((bf16[8,512,256]{2,1,0:T(8,128)(2,1)}), bf16[8,512,256]{2,1,0:T(8,128)(2,1)}, u32[]{:S(2)}, u32[]{:S(2)}) async-start(bf16[8,512,256]{2,1,0:T(8,128)(2,1)} %bitcast.42), calls=%async_computation.2 | async-start | bytes 4194304 | tf_op jit(solution)/shard_map/all_to_all | solution.py:190
  198.5 1.2 copy-done.2
  199.7 14.1 %attend.5.refs_4_ = bf16[768,256]{1,0:T(8,128)(2,1)S(1)} custom-call(s32[192]{0:T(256)S(1)} %fusion.14.place_ref, bf16[768,640]{1,0:T(8,128)(2,1)S(1)} %copy-done.2, bf16[768,640]{1,0:T(8,128)(2,1)S(1)} %copy-done.2, bf16[4096,512]{1,0:T(8,128)(2,1)} %bitcast.5.refs_2_.refs_3_, bf16[4096,512]{1,0:T(8,128)(2,1)} %bitcast.5.refs_2_.refs_3_), custom_call_target="tpu_custom_call" | custom-call | flops 805306368 | bytes 4194304 | tf_op jit(solution)/shard_map/attend/pallas_call | solution.py:97
  213.8 0.7 copy-done.11
  214.6 8.9 %all-gather.16.cloned.1.call-done.refs_0_ = bf16[6144,256]{1,0:T(8,128)(2,1)} async-done(((bf16[768,256]{1,0:T(8,128)(2,1)}), bf16[6144,256]{1,0:T(8,128)(2,1)}) %all-gather.16.cloned.1.call-update) | async-done | bytes 3145744 | tf_op jit(solution)/shard_map/all_gather | solution.py:224
  223.4 1.9 copy-done.10
  225.3 0.8 pick.7
  226.1 1.3 copy-done.6
  227.5 5.3 %all-to-all-start.3 = ((bf16[8,512,256]{2,1,0:T(8,128)(2,1)}), bf16[8,512,256]{2,1,0:T(8,128)(2,1)}, u32[]{:S(2)}, u32[]{:S(2)}) async-start(bf16[8,512,256]{2,1,0:T(8,128)(2,1)} %bitcast.41), calls=%async_computation.3 | async-start | bytes 4194304 | tf_op jit(solution)/shard_map/all_to_all | solution.py:190
  232.7 2.4 collective-permute-start.11
  235.1 0.6 collective-permute-start.10
  235.7 0.6 collective-permute-start.9
  236.3 1.2 copy-done.3
  237.5 8.4 %attend.6.refs_8_ = bf16[768,128]{1,0:T(8,128)(2,1)} custom-call(s32[192]{0:T(256)S(1)} %fusion.14.place_ref, bf16[768,640]{1,0:T(8,128)(2,1)S(1)} %copy-done.3, bf16[4096,256]{1,0:T(8,128)(2,1)} %bitcast.7.refs_1_), custom_call_target="tpu_custom_call" | custom-call | flops 402653184 | bytes 2097152 | tf_op jit(solution)/shard_map/attend/pallas_call | solution.py:97
  245.9 2.1 collective-permute-start.14
  248.0 1.2 collective-permute-start.13
  249.2 2.5 collective-permute-done.11.refs_7_
  251.8 0.8 copy-done.13
  252.5 6.7 %all-to-all-done.3 = bf16[8,512,256]{2,1,0:T(8,128)(2,1)} async-done(((bf16[8,512,256]{2,1,0:T(8,128)(2,1)}), bf16[8,512,256]{2,1,0:T(8,128)(2,1)}, u32[]{:S(2)}, u32[]{:S(2)}) %all-to-all-start.3) | async-done | bytes 2097184 | tf_op jit(solution)/shard_map/all_to_all | solution.py:190
  259.2 1.2 copy-done.4
  260.4 7.8 %attend.7.refs_0_ = bf16[768,128]{1,0:T(8,128)(2,1)S(1)} custom-call(s32[192]{0:T(256)S(1)} %fusion.14.place_ref, bf16[768,640]{1,0:T(8,128)(2,1)S(1)} %copy-done.4, bf16[4096,256]{1,0:T(8,128)(2,1)} %bitcast.9.refs_1_), custom_call_target="tpu_custom_call" | custom-call | flops 402653184 | bytes 2097152 | tf_op jit(solution)/shard_map/attend/pallas_call | solution.py:97
  268.2 2.5 collective-permute-start.8
  270.7 0.6 collective-permute-start.7
  271.3 0.6 collective-permute-start.6
  271.9 7.9 %project.2.refs_8_ = f32[768,1280]{1,0:T(8,128)S(1)} custom-call(bf16[768,128]{1,0:T(8,128)(2,1)S(1)} %attend.4.refs_0_, bf16[768,128]{1,0:T(8,128)(2,1)S(1)} %copy-done.20, bf16[768,128]{1,0:T(8,128)(2,1)S(1)} %copy-done.18, bf16[768,128]{1,0:T(8,128)(2,1)S(1)} %copy-done.16, bf16[768,256]{1,0:T(8,128)(2,1)S(1)} %copy-done.12, ...), custom_call_target="tpu_custom_call" | custom-call | flops 4026531840 | bytes 10354688 | tf_op jit(solution)/shard_map/project/pallas_call | solution.py:156
  279.9 3.3 %collective-permute-done.6.refs_1_ = bf16[768,128]{1,0:T(8,128)(2,1)S(1)} collective-permute-done((bf16[768,128]{1,0:T(8,128)(2,1)S(1)}, bf16[768,128]{1,0:T(8,128)(2,1)S(1)}, u32[]{:S(2)}, u32[]{:S(2)}) %collective-permute-start.6) | collective-permute-done | bytes 196640 | tf_op jit(solution)/shard_map/ppermute | solution.py:220
  283.2 4.9 %project.3 = bf16[768,1280]{1,0:T(8,128)(2,1)} custom-call(bf16[768,128]{1,0:T(8,128)(2,1)S(1)} %attend.7.refs_0_, bf16[768,128]{1,0:T(8,128)(2,1)S(1)} %collective-permute-done.6.refs_1_, bf16[768,128]{1,0:T(8,128)(2,1)S(1)} %collective-permute-done.7.refs_2_, bf16[768,128]{1,0:T(8,128)(2,1)S(1)} %collective-permute-done.8.refs_3_, ...), custom_call_target="tpu_custom_call" | custom-call | flops 1006632960 | bytes 4063232 | tf_op jit(solution)/shard_map/project/pallas_call | solution.py:156
  (65 shorter events, 1.6 us)
Async XLA Ops:
  6.5 1.6 copy-start.21
  6.5 51.3 %all-gather.10.cloned.1.call-start = ((), (), s32[]{:S(2)}) async-start(), calls=%async_computation.4 | async-start | bytes 3538944 | tf_op jit(solution)/shard_map/all_gather | solution.py:224
  8.3 2.0 copy-start.22
  8.4 2.0 copy-start.23
  9.2 123.9 %all-gather.12.cloned.1.call-start = ((), (), s32[]{:S(2)}) async-start(), calls=%async_computation.5 | async-start | bytes 7077888 | tf_op jit(solution)/shard_map/all_gather | solution.py:224
  10.2 168.0 %all-gather.14.cloned.1.call-start = ((), (), s32[]{:S(2)}) async-start(), calls=%async_computation.6 | async-start | bytes 3538944 | tf_op jit(solution)/shard_map/all_gather | solution.py:224
  57.9 1.9 copy-start.9
  62.0 31.6 %all-to-all-start = ((bf16[8,512,256]{2,1,0:T(8,128)(2,1)}), bf16[8,512,256]{2,1,0:T(8,128)(2,1)}, u32[]{:S(2)}, u32[]{:S(2)}) async-start(bf16[8,512,256]{2,1,0:T(8,128)(2,1)} %bitcast.2), calls=%async_computation | async-start | bytes 4194304 | tf_op jit(solution)/shard_map/all_to_all | solution.py:190
  72.5 37.9 %collective-permute-start.4 = (bf16[640,1280]{1,0:T(8,128)(2,1)}, bf16[640,1280]{1,0:T(8,128)(2,1)S(1)}, u32[]{:S(2)}, u32[]{:S(2)}) collective-permute-start(bf16[640,1280]{1,0:T(8,128)(2,1)} %get-tuple-element.52), channel_id=1, source_target_pairs={{0,3},{1,0},{2,1},{3,2},{4,7},{5,4},{6,5},{7,6},{8,11},{9,8},{10,9... | collective-permute-start | bytes 4915208 | tf_op jit(solution)/shard_map/ppermute | solution.py:217
  74.9 42.0 %collective-permute-start.3 = (bf16[640,1280]{1,0:T(8,128)(2,1)}, bf16[640,1280]{1,0:T(8,128)(2,1)}, u32[]{:S(2)}, u32[]{:S(2)}) collective-permute-start(bf16[640,1280]{1,0:T(8,128)(2,1)} %get-tuple-element.53), channel_id=1, source_target_pairs={{0,1},{1,2},{2,3},{3,0},{4,5},{5,6},{6,7},{7,4},{8,9},{9,10},{10,1... | collective-permute-start | bytes 4915208 | tf_op jit(solution)/shard_map/ppermute | solution.py:217
  93.7 1.2 copy-start.1
  102.7 15.9 %collective-permute-start.2 = (bf16[768,128]{1,0:T(8,128)(2,1)S(1)}, bf16[768,128]{1,0:T(8,128)(2,1)S(1)}, u32[]{:S(2)}, u32[]{:S(2)}) collective-permute-start(bf16[768,128]{1,0:T(8,128)(2,1)S(1)} %attend.4.refs_0_), channel_id=1, source_target_pairs={{0,3},{1,0},{2,1},{3,2},{4,7},{5,4},{6,5},{7,6},{8,11},{9,8},{10,9... | collective-permute-start | bytes 589832 | tf_op jit(solution)/shard_map/ppermute | solution.py:220
  105.2 14.1 %collective-permute-start.1 = (bf16[768,128]{1,0:T(8,128)(2,1)S(1)}, bf16[768,128]{1,0:T(8,128)(2,1)S(1)}, u32[]{:S(2)}, u32[]{:S(2)}) collective-permute-start(bf16[768,128]{1,0:T(8,128)(2,1)S(1)} %attend.4.refs_0_), channel_id=1, source_target_pairs={{0,2},{1,3},{2,0},{3,1},{4,6},{5,7},{6,4},{7,5},{8,10},{9,11},{10,... | collective-permute-start | bytes 589832 | tf_op jit(solution)/shard_map/ppermute | solution.py:220
  105.8 16.1 %collective-permute-start = (bf16[768,128]{1,0:T(8,128)(2,1)S(1)}, bf16[768,128]{1,0:T(8,128)(2,1)S(1)}, u32[]{:S(2)}, u32[]{:S(2)}) collective-permute-start(bf16[768,128]{1,0:T(8,128)(2,1)S(1)} %attend.4.refs_0_), channel_id=1, source_target_pairs={{0,1},{1,2},{2,3},{3,0},{4,5},{5,6},{6,7},{7,4},{8,9},{9,10},{10,1... | collective-permute-start | bytes 589832 | tf_op jit(solution)/shard_map/ppermute | solution.py:220
  118.6 0.7 copy-start.15
  119.3 0.7 copy-start.17
  121.9 0.7 copy-start.19
  133.0 2.8 copy-start
  137.3 2.0 copy-start.5
  139.3 54.0 %all-to-all-start.1 = ((bf16[8,512,512]{2,1,0:T(8,128)(2,1)}), bf16[8,512,512]{2,1,0:T(8,128)(2,1)}, u32[]{:S(2)}, u32[]{:S(2)}) async-start(bf16[8,512,512]{2,1,0:T(8,128)(2,1)} %bitcast.40), calls=%async_computation.1 | async-start | bytes 8388608 | tf_op jit(solution)/shard_map/all_to_all | solution.py:190
  144.4 79.0 %all-gather.16.cloned.1.call-start = ((), (), s32[]{:S(2)}) async-start(), calls=%async_computation.7 | async-start | bytes 3538944 | tf_op jit(solution)/shard_map/all_gather | solution.py:224
  145.0 39.2 %collective-permute-start.5 = (bf16[640,1280]{1,0:T(8,128)(2,1)}, bf16[640,1280]{1,0:T(8,128)(2,1)}, u32[]{:S(2)}, u32[]{:S(2)}) collective-permute-start(bf16[640,1280]{1,0:T(8,128)(2,1)} %get-tuple-element.54), channel_id=1, source_target_pairs={{0,2},{1,3},{2,0},{3,1},{4,6},{5,7},{6,4},{7,5},{8,10},{9,11},{10,... | collective-permute-start | bytes 4915208 | tf_op jit(solution)/shard_map/ppermute | solution.py:217
  178.2 1.9 copy-start.8
  180.9 1.3 copy-start.7
  193.3 34.1 %all-to-all-start.2 = ((bf16[8,512,256]{2,1,0:T(8,128)(2,1)}), bf16[8,512,256]{2,1,0:T(8,128)(2,1)}, u32[]{:S(2)}, u32[]{:S(2)}) async-start(bf16[8,512,256]{2,1,0:T(8,128)(2,1)} %bitcast.42), calls=%async_computation.2 | async-start | bytes 4194304 | tf_op jit(solution)/shard_map/all_to_all | solution.py:190
  198.4 1.2 copy-start.2
  213.8 0.7 copy-start.11
  223.4 1.9 copy-start.10
  226.1 1.3 copy-start.6
  227.5 31.7 %all-to-all-start.3 = ((bf16[8,512,256]{2,1,0:T(8,128)(2,1)}), bf16[8,512,256]{2,1,0:T(8,128)(2,1)}, u32[]{:S(2)}, u32[]{:S(2)}) async-start(bf16[8,512,256]{2,1,0:T(8,128)(2,1)} %bitcast.41), calls=%async_computation.3 | async-start | bytes 4194304 | tf_op jit(solution)/shard_map/all_to_all | solution.py:190
  232.7 19.0 %collective-permute-start.11 = (bf16[768,256]{1,0:T(8,128)(2,1)}, bf16[768,256]{1,0:T(8,128)(2,1)S(1)}, u32[]{:S(2)}, u32[]{:S(2)}) collective-permute-start(bf16[768,256]{1,0:T(8,128)(2,1)} %copy-done.11), channel_id=1, source_target_pairs={{0,3},{1,0},{2,1},{3,2},{4,7},{5,4},{6,5},{7,6},{8,11},{9,8},{10,9... | collective-permute-start | bytes 1179656 | tf_op jit(solution)/shard_map/ppermute | solution.py:220
  235.1 33.0 %collective-permute-start.10 = (bf16[768,256]{1,0:T(8,128)(2,1)}, bf16[768,256]{1,0:T(8,128)(2,1)}, u32[]{:S(2)}, u32[]{:S(2)}) collective-permute-start(bf16[768,256]{1,0:T(8,128)(2,1)} %copy-done.11), channel_id=1, source_target_pairs={{0,2},{1,3},{2,0},{3,1},{4,6},{5,7},{6,4},{7,5},{8,10},{9,11},{10,... | collective-permute-start | bytes 1179656 | tf_op jit(solution)/shard_map/ppermute | solution.py:220
  235.7 35.0 %collective-permute-start.9 = (bf16[768,256]{1,0:T(8,128)(2,1)}, bf16[768,256]{1,0:T(8,128)(2,1)}, u32[]{:S(2)}, u32[]{:S(2)}) collective-permute-start(bf16[768,256]{1,0:T(8,128)(2,1)} %copy-done.11), channel_id=1, source_target_pairs={{0,1},{1,2},{2,3},{3,0},{4,5},{5,6},{6,7},{7,4},{8,9},{9,10},{10,1... | collective-permute-start | bytes 1179656 | tf_op jit(solution)/shard_map/ppermute | solution.py:220
  236.3 1.2 copy-start.3
  245.9 25.3 %collective-permute-start.14 = (bf16[768,128]{1,0:T(8,128)(2,1)}, bf16[768,128]{1,0:T(8,128)(2,1)}, u32[]{:S(2)}, u32[]{:S(2)}) collective-permute-start(bf16[768,128]{1,0:T(8,128)(2,1)} %attend.6.refs_8_), channel_id=1, source_target_pairs={{0,3},{1,0},{2,1},{3,2},{4,7},{5,4},{6,5},{7,6},{8,11},{9,8},{10,9... | collective-permute-start | bytes 589832 | tf_op jit(solution)/shard_map/ppermute | solution.py:220
  248.0 23.9 %collective-permute-start.13 = (bf16[768,128]{1,0:T(8,128)(2,1)}, bf16[768,128]{1,0:T(8,128)(2,1)}, u32[]{:S(2)}, u32[]{:S(2)}) collective-permute-start(bf16[768,128]{1,0:T(8,128)(2,1)} %attend.6.refs_8_), channel_id=1, source_target_pairs={{0,2},{1,3},{2,0},{3,1},{4,6},{5,7},{6,4},{7,5},{8,10},{9,11},{10,... | collective-permute-start | bytes 589832 | tf_op jit(solution)/shard_map/ppermute | solution.py:220
  251.8 0.8 copy-start.13
  252.5 19.4 %collective-permute-start.12 = (bf16[768,128]{1,0:T(8,128)(2,1)}, bf16[768,128]{1,0:T(8,128)(2,1)}, u32[]{:S(2)}, u32[]{:S(2)}) collective-permute-start(bf16[768,128]{1,0:T(8,128)(2,1)} %attend.6.refs_8_), channel_id=1, source_target_pairs={{0,1},{1,2},{2,3},{3,0},{4,5},{5,6},{6,7},{7,4},{8,9},{9,10},{10,1... | collective-permute-start | bytes 589832 | tf_op jit(solution)/shard_map/ppermute | solution.py:220
  259.2 1.2 copy-start.4
  260.4 11.5 %copy-start.12 = (bf16[768,256]{1,0:T(8,128)(2,1)S(1)}, bf16[768,256]{1,0:T(8,128)(2,1)}, u32[]{:S(2)}) copy-start(bf16[768,256]{1,0:T(8,128)(2,1)} %copy-done.11) | copy-start | bytes 1179652
  260.4 11.5 %copy-start.14 = (bf16[768,256]{1,0:T(8,128)(2,1)S(1)}, bf16[768,256]{1,0:T(8,128)(2,1)}, u32[]{:S(2)}) copy-start(bf16[768,256]{1,0:T(8,128)(2,1)} %copy-done.13) | copy-start | bytes 1179652
  260.4 11.5 %copy-start.16 = (bf16[768,128]{1,0:T(8,128)(2,1)S(1)}, bf16[768,128]{1,0:T(8,128)(2,1)}, u32[]{:S(2)}) copy-start(bf16[768,128]{1,0:T(8,128)(2,1)} %copy-done.15) | copy-start | bytes 589828
  260.4 11.5 %copy-start.18 = (bf16[768,128]{1,0:T(8,128)(2,1)S(1)}, bf16[768,128]{1,0:T(8,128)(2,1)}, u32[]{:S(2)}) copy-start(bf16[768,128]{1,0:T(8,128)(2,1)} %copy-done.17) | copy-start | bytes 589828
  260.4 11.5 %copy-start.20 = (bf16[768,128]{1,0:T(8,128)(2,1)S(1)}, bf16[768,128]{1,0:T(8,128)(2,1)}, u32[]{:S(2)}) copy-start(bf16[768,128]{1,0:T(8,128)(2,1)} %copy-done.19) | copy-start | bytes 589828
  268.2 11.7 %collective-permute-start.8 = (bf16[768,128]{1,0:T(8,128)(2,1)S(1)}, bf16[768,128]{1,0:T(8,128)(2,1)S(1)}, u32[]{:S(2)}, u32[]{:S(2)}) collective-permute-start(bf16[768,128]{1,0:T(8,128)(2,1)S(1)} %attend.7.refs_0_), channel_id=1, source_target_pairs={{0,3},{1,0},{2,1},{3,2},{4,7},{5,4},{6,5},{7,6},{8,11},{9,8},{10,9... | collective-permute-start | bytes 589832 | tf_op jit(solution)/shard_map/ppermute | solution.py:220
  270.7 9.2 %collective-permute-start.7 = (bf16[768,128]{1,0:T(8,128)(2,1)S(1)}, bf16[768,128]{1,0:T(8,128)(2,1)S(1)}, u32[]{:S(2)}, u32[]{:S(2)}) collective-permute-start(bf16[768,128]{1,0:T(8,128)(2,1)S(1)} %attend.7.refs_0_), channel_id=1, source_target_pairs={{0,2},{1,3},{2,0},{3,1},{4,6},{5,7},{6,4},{7,5},{8,10},{9,11},{10,... | collective-permute-start | bytes 589832 | tf_op jit(solution)/shard_map/ppermute | solution.py:220
  271.3 12.0 %collective-permute-start.6 = (bf16[768,128]{1,0:T(8,128)(2,1)S(1)}, bf16[768,128]{1,0:T(8,128)(2,1)S(1)}, u32[]{:S(2)}, u32[]{:S(2)}) collective-permute-start(bf16[768,128]{1,0:T(8,128)(2,1)S(1)} %attend.7.refs_0_), channel_id=1, source_target_pairs={{0,1},{1,2},{2,3},{3,0},{4,5},{5,6},{6,7},{7,4},{8,9},{9,10},{10,1... | collective-permute-start | bytes 589832 | tf_op jit(solution)/shard_map/ppermute | solution.py:220
Sparse Core Ops, SparseCore 0:
  9.3 48.5 all-gather.9
  59.7 73.3 all-gather.11
  134.8 43.3 all-gather.13
  179.9 43.5 all-gather.15

commit v3 on v2

--- a/solution.py
+++ b/solution.py
@@ -208,6 +208,7 @@
     matches = mine[:, None, :] & (step[:, None, :] == steps)
     want = jnp.max(jnp.where(matches, plane[:, None, :] % cubes_here, 0), axis=2)
     from_z = (z - steps[:, 0]) % NZ * cubes_here
+    want_ring = (want + steps[:, 0] * cubes_here).reshape(-1)
     want = (want + from_z).reshape(-1)
 
     w_columns = width_out = w_out.shape[1] // groups
@@ -223,6 +224,17 @@
         (chunk,) = after((pack(heads),), earlier)
         return lax.all_gather(chunk, "z", axis=0).reshape(NZ * tokens, -1)
 
+    def ring(chunk):
+        far = tokens // 2
+        ups, downs = [chunk], [chunk]
+        for s in range(4):
+            up, down = ups[-1], downs[-1]
+            if s == 3:
+                up, down = up[:far], down[far:]
+            ups.append(lax.ppermute(up, "z", shift(NZ, 1)))
+            downs.append(lax.ppermute(down, "z", shift(NZ, -1)))
+        return jnp.concatenate(ups + downs[:0:-1], axis=0)
+
     g0 = gather((0,))
     g12 = gather((1, 2))
 
@@ -230,33 +242,33 @@
     out0 = pick(want, g0, 0, 1)
     in0 = exchange(out0)
     g3 = gather((3,), (out0,))
+    g4 = ring(after((pack((4,)),), (out0,))[0])
     rows0 = attend(places, queries, [(in0, 0)], 0)
     all0 = spread(rows0)
 
+    (g4,) = after((g4,), (rows0,))
+    in4 = exchange(pick(want_ring, g4, 0, 1))
     (g12,) = after((g12,), all0[1:] + [weights[1], weights[3]])
     out12 = pick(want, g12, 0, 2)
+    in4, out12 = after((in4, out12), ())
     in12 = exchange(out12)
-    g4 = gather((4,), (out12,))
+    rows4 = attend(places, queries, [(in4, 0)], 4)
+    all4 = spread(rows4)
+
+    g3, _ = after((g3, rows4), ())
     out3 = pick(want, g3, 0, 1)
-    in12, out3 = after((in12, out3), (weights[2],))
+    in12, out3 = after((in12, out3), [weights[2]] + all4[1:])
     in3 = exchange(out3)
     rows12 = attend(places, queries, [(in12, 0), (in12, 1)], 1)
     all12 = spread(rows12)
 
-    g4, _ = after((g4, rows12), ())
-    out4 = pick(want, g4, 0, 1)
-    in3, out4 = after((in3, out4), ())
-    in4 = exchange(out4)
+    (in3,) = after((in3,), (rows12,))
     rows3 = attend(places, queries, [(in3, 0)], 3)
     all3 = spread(rows3)
-
-    (in4,) = after((in4,), (rows3,))
-    rows4 = attend(places, queries, [(in4, 0)], 4)
-    all4 = spread(rows4)
-    held = after(all0 + all12 + all3, (rows4,))
-    terms = [(held[:groups], 0), (held[groups : 2 * groups], 1), (held[2 * groups :], 3)]
+    held = after(all0 + all12 + all4, (rows3,))
+    terms = [(held[:groups], 0), (held[groups : 2 * groups], 1), (held[2 * groups :], 4)]
     total = project(terms, weights, None, jnp.float32)
-    return project([(all4, 4)], weights, total, jnp.bfloat16)
+    return project([(all3, 3)], weights, total, jnp.bfloat16)
 
 
 def solution(mesh):

time: 296 us -> 329 us (1.11)
  starting transfers between devices: 40.2 us -> 60.4 us
  waiting for transfers between devices: 140 us -> 148 us
  local copies, waits for them, and re-layouts: 28.9 us -> 34.8 us
    all_gather x4 -> x3, waiting for transfers between devices: 83.4 us -> 33.8 us  [gather(): return lax.all_gather(chunk, 'z', axis=0).reshape(NZ * tokens, -1)]
    ppermute x3, waiting for transfers between devices: 12.6 us -> 52.2 us  [per_device(): weights.append(lax.ppermute(part, 'head', shift(groups, d)) if d else part)]
    ppermute x0 -> x8, waiting for transfers between devices: none -> 39.2 us  [the longest x4 37.1 us: ring(): ups.append(lax.ppermute(up, 'z', shift(NZ, 1)))]
    all_to_all x4, waiting for transfers between devices: 34.4 us -> 6.75 us  [exchange(): lax.all_to_all(outgoing, ('y', 'core'), split_axis=0, concat_axis=0, tile...]
    ppermute x0 -> x8, starting transfers between devices: none -> 12.5 us  [the longest x4 12.4 us: ring(): downs.append(lax.ppermute(down, 'z', shift(NZ, -1)))]
    ppermute x12, waiting for transfers between devices: 9.48 us -> 16.1 us  [spread(): lax.ppermute(rows, 'head', shift(groups, d))]
    all_to_all x4, starting transfers between devices: 20.7 us -> 27.2 us  [exchange(): lax.all_to_all(outgoing, ('y', 'core'), split_axis=0, concat_axis=0, tile...]
    unnamed x49 -> x59, local copies, waits for them, and re-layouts: 21.7 us -> 25.3 us
  transfers between devices with their start and end apart: 23 -> 30, of which waited for: 14 -> 18; matrix products, arithmetic and copies ran while one was open for 3% -> 4% of each run, Pallas kernels for 17% -> 15%
where the time goes in v3:
time: 329 us; the launch traced here: 327 us
  waiting for transfers between devices  148 us (45%)
  starting transfers between devices  60.4 us (18%)
  Pallas kernels  55.1 us (17%)
  local copies, waits for them, and re-layouts  34.8 us (11%)
  between operations  13.5 us (4%)
  blocking collectives  12.1 us (4%)
  other arithmetic  3.33 us (1%)
    ppermute x3, waiting for transfers between devices, per_device(): weights.append(lax.ppermute(part, 'head', shift(groups, d)) if d else part)  52.2 us
    ppermute x4, waiting for transfers between devices, ring(): ups.append(lax.ppermute(up, 'z', shift(NZ, 1)))  37.1 us
    pallas_call x4, Pallas kernels, attend(): pl.pallas_call(functools.partial(attend_kernel, cubes=cubes, per=per), ou...  37.1 us
    all_gather x3, waiting for transfers between devices, gather(): return lax.all_gather(chunk, 'z', axis=0).reshape(NZ * tokens, -1)  33.8 us
    all_to_all x4, starting transfers between devices, exchange(): lax.all_to_all(outgoing, ('y', 'core'), split_axis=0, concat_axis=0, tile...  27.2 us
    unnamed x59, local copies, waits for them, and re-layouts  25.3 us
    ppermute x12, starting transfers between devices, spread(): lax.ppermute(rows, 'head', shift(groups, d))  17.4 us
    ppermute x12, waiting for transfers between devices, spread(): lax.ppermute(rows, 'head', shift(groups, d))  16.1 us
  transfers between devices with their start and end apart: 30, of which 18 were waited for; matrix products, arithmetic and copies ran while one was open for 4% of the time, Pallas kernels for 15%

profile of v3, /device:TPU:1, one launch (start us, length us, event | category | flops | bytes accessed | tf_op | source)
XLA Modules:
  0.0 327.4 jit_solution(11524082635126184248)
XLA Ops:
  6.5 1.4 fusion.21
  7.9 1.4 fusion.22
  10.2 1.0 pad_maximum_fusion
  11.6 12.1 %all-gather.3 = s32[8,1,192]{2,1,0:T(1,128)S(1)} all-gather(s32[1,1,192]{2,1,0:T(1,128)S(1)} %reshape.76), channel_id=1, replica_groups=mesh['y'=4,'z'=8,'core'=2,'head'=4] {'y','core'}, dimensions={0}, use_global_device_ids=true | all-gather | bytes 6912 | tf_op jit(solution)/shard_map/all_gather | solution.py:203
  24.2 0.8 pad_maximum_fusion.1
  25.0 33.8 %all-gather.8.cloned.1.call-done.refs_0_ = bf16[6144,256]{1,0:T(8,128)(2,1)} async-done(((bf16[768,256]{1,0:T(8,128)(2,1)}), bf16[6144,256]{1,0:T(8,128)(2,1)}) %all-gather.8.cloned.1.call-update) | async-done | bytes 3145744 | tf_op jit(solution)/shard_map/all_gather | solution.py:225
  58.8 1.9 copy-done.13
  61.5 1.4 copy-done.8
  62.9 2.7 collective-permute-start.4
  65.6 5.8 %all-to-all-start = ((bf16[8,512,256]{2,1,0:T(8,128)(2,1)}), bf16[8,512,256]{2,1,0:T(8,128)(2,1)S(1)}, u32[]{:S(2)}, u32[]{:S(2)}) async-start(bf16[8,512,256]{2,1,0:T(8,128)(2,1)} %bitcast.42), calls=%async_computation | async-start | bytes 4194304 | tf_op jit(solution)/shard_map/all_to_all | solution.py:190
  71.3 2.5 collective-permute-done
  74.7 3.5 %collective-permute-start.5 = (bf16[768,256]{1,0:T(8,128)(2,1)S(1)}, bf16[768,256]{1,0:T(8,128)(2,1)}, u32[]{:S(2)}, u32[]{:S(2)}) collective-permute-start(bf16[768,256]{1,0:T(8,128)(2,1)S(1)} %collective-permute-done.4), channel_id=1, source_target_pairs={{0,56},{8,0},{16,8},{24,16},{32,24},{40,32},{48,40},{56,48},{1,57}... | collective-permute-start | bytes 1179656 | tf_op jit(solution)/shard_map/ppermute | solution.py:235
  78.4 15.2 %collective-permute-done.1 = bf16[768,256]{1,0:T(8,128)(2,1)} collective-permute-done((bf16[768,256]{1,0:T(8,128)(2,1)S(1)}, bf16[768,256]{1,0:T(8,128)(2,1)}, u32[]{:S(2)}, u32[]{:S(2)}) %collective-permute-start.1) | collective-permute-done | bytes 393248 | tf_op jit(solution)/shard_map/ppermute | solution.py:234
  93.9 3.5 %collective-permute-start.6 = (bf16[768,256]{1,0:T(8,128)(2,1)}, bf16[768,256]{1,0:T(8,128)(2,1)}, u32[]{:S(2)}, u32[]{:S(2)}) collective-permute-start(bf16[768,256]{1,0:T(8,128)(2,1)} %collective-permute-done.5), channel_id=1, source_target_pairs={{0,56},{8,0},{16,8},{24,16},{32,24},{40,32},{48,40},{56,48},{1,57}... | collective-permute-start | bytes 1179656 | tf_op jit(solution)/shard_map/ppermute | solution.py:235
  97.7 1.1 constant_dynamic-update-slice_fusion.7
  98.8 14.4 %collective-permute-done.2 = bf16[768,256]{1,0:T(8,128)(2,1)} collective-permute-done((bf16[768,256]{1,0:T(8,128)(2,1)}, bf16[768,256]{1,0:T(8,128)(2,1)}, u32[]{:S(2)}, u32[]{:S(2)}) %collective-permute-start.2) | collective-permute-done | bytes 393248 | tf_op jit(solution)/shard_map/ppermute | solution.py:234
  113.2 0.9 slice.48
  114.3 1.0 constant_dynamic-update-slice_fusion.6
  115.3 0.9 slice.49
  116.3 2.7 collective-permute-start.7
  119.0 1.0 constant_dynamic-update-slice_fusion.5
  120.0 5.0 %collective-permute-done.3 = bf16[384,256]{1,0:T(8,128)(2,1)S(1)} collective-permute-done((bf16[384,256]{1,0:T(8,128)(2,1)S(1)}, bf16[384,256]{1,0:T(8,128)(2,1)S(1)}, u32[]{:S(2)}, u32[]{:S(2)}) %collective-permute-start.3) | collective-permute-done | bytes 196640 | tf_op jit(solution)/shard_map/ppermute | solution.py:234
  125.0 1.0 collective-permute-done.7
  126.0 1.0 constant_dynamic-update-slice_fusion.2
  127.0 1.0 constant_dynamic-update-slice_fusion.1
  128.1 1.7 copy-done.10
  129.8 6.1 %attend.4.refs_0_ = bf16[768,128]{1,0:T(8,128)(2,1)S(1)} custom-call(s32[192]{0:T(256)S(1)} %fusion.14.place_ref, bf16[768,640]{1,0:T(8,128)(2,1)S(1)} %copy-done.3, bf16[4096,256]{1,0:T(8,128)(2,1)S(1)} %bitcast.41), custom_call_target="tpu_custom_call" | custom-call | flops 402653184 | bytes 2097152 | tf_op jit(solution)/shard_map/attend/pallas_call | solution.py:97
  135.9 2.1 pick.5
  138.0 11.1 %all-to-all-start.1 = ((bf16[8,512,256]{2,1,0:T(8,128)(2,1)}), bf16[8,512,256]{2,1,0:T(8,128)(2,1)}, u32[]{:S(2)}, u32[]{:S(2)}) async-start(bf16[8,512,256]{2,1,0:T(8,128)(2,1)} %bitcast.4), calls=%async_computation.1 | async-start | bytes 4194304 | tf_op jit(solution)/shard_map/all_to_all | solution.py:190
  149.1 4.5 %constant_dynamic-slice_fusion.3 = (bf16[640,1280]{1,0:T(8,128)(2,1)S(1)}, bf16[640,1280]{1,0:T(8,128)(2,1)S(1)}, bf16[640,1280]{1,0:T(8,128)(2,1)S(1)}, bf16[640,1280]{1,0:T(8,128)(2,1)}) fusion(bf16[640,5120]{1,0:T(8,128)(2,1)} %param.9, s32[]{:T(128)S(6)} %select_n.129, s32[]{:T(128)S(6)} %select_n.125, s32[]{:T(128)S(6)} %select_n.123, s32[]{:T(128)S(6)} %select_n.127), kind=kLoop, calls=%fused_computation.83 | loop fusion | bytes 13107216 | tf_op jit(solution)/shard_map/dynamic_slice | solution.py:217
  153.6 1.1 collective-permute-start.11
  154.7 1.6 collective-permute-start.12
  156.3 1.1 collective-permute-start.10
  157.8 1.4 collective-permute-start.9
  159.2 33.0 %collective-permute-done.11.refs_13_.refs_18_.refs_19_.refs_25_.refs_5_ = bf16[640,1280]{1,0:T(8,128)(2,1)S(1)} collective-permute-done((bf16[640,1280]{1,0:T(8,128)(2,1)S(1)}, bf16[640,1280]{1,0:T(8,128)(2,1)S(1)}, u32[]{:S(2)}, u32[]{:S(2)}) %collective-permute-start.11) | collective-permute-done | bytes 1638432 | tf_op jit(solution)/shard_map/ppermute | solution.py:218
  192.2 1.2 copy-done
  193.4 2.7 collective-permute-done.10.refs_3_
  197.5 4.0 %collective-permute-done.9.refs_2_ = bf16[768,128]{1,0:T(8,128)(2,1)S(1)} collective-permute-done((bf16[768,128]{1,0:T(8,128)(2,1)S(1)}, bf16[768,128]{1,0:T(8,128)(2,1)S(1)}, u32[]{:S(2)}, u32[]{:S(2)}) %collective-permute-start.9) | collective-permute-done | bytes 196640 | tf_op jit(solution)/shard_map/ppermute | solution.py:221
  202.2 2.8 copy-done.2
  204.9 1.5 pick.6
  206.4 2.0 copy-done.7
  208.4 5.3 %all-to-all-start.2 = ((bf16[8,512,512]{2,1,0:T(8,128)(2,1)}), bf16[8,512,512]{2,1,0:T(8,128)(2,1)}, u32[]{:S(2)}, u32[]{:S(2)}) async-start(bf16[8,512,512]{2,1,0:T(8,128)(2,1)} %bitcast.40), calls=%async_computation.2 | async-start | bytes 8388608 | tf_op jit(solution)/shard_map/all_to_all | solution.py:190
  214.3 1.2 copy-done.4
  215.5 8.4 %attend.5.refs_8_ = bf16[768,128]{1,0:T(8,128)(2,1)} custom-call(s32[192]{0:T(256)S(1)} %fusion.14.place_ref, bf16[768,640]{1,0:T(8,128)(2,1)S(1)} %copy-done.4, bf16[4096,256]{1,0:T(8,128)(2,1)} %bitcast.5.refs_1_), custom_call_target="tpu_custom_call" | custom-call | flops 402653184 | bytes 2097152 | tf_op jit(solution)/shard_map/attend/pallas_call | solution.py:97
  223.9 3.2 collective-permute-start.14
  227.8 1.8 collective-permute-start.16
  229.6 1.9 copy-done.12
  232.2 1.3 copy-done.9
  233.6 19.2 %collective-permute-done.13.refs_14_.refs_20_.refs_21_.refs_26_.refs_6_ = bf16[640,1280]{1,0:T(8,128)(2,1)} collective-permute-done((bf16[640,1280]{1,0:T(8,128)(2,1)}, bf16[640,1280]{1,0:T(8,128)(2,1)}, u32[]{:S(2)}, u32[]{:S(2)}) %collective-permute-start.13) | collective-permute-done | bytes 1638432 | tf_op jit(solution)/shard_map/ppermute | solution.py:218
  252.8 5.2 %collective-permute-done.14.refs_9_ = bf16[768,128]{1,0:T(8,128)(2,1)} collective-permute-done((bf16[768,128]{1,0:T(8,128)(2,1)}, bf16[768,128]{1,0:T(8,128)(2,1)}, u32[]{:S(2)}, u32[]{:S(2)}) %collective-permute-start.14) | collective-permute-done | bytes 196640 | tf_op jit(solution)/shard_map/ppermute | solution.py:221
  258.0 3.2 collective-permute-done.15.refs_10_
  261.2 0.9 collective-permute-done.16.refs_11_
  262.7 5.1 %all-to-all-start.3 = ((bf16[8,512,256]{2,1,0:T(8,128)(2,1)}), bf16[8,512,256]{2,1,0:T(8,128)(2,1)}, u32[]{:S(2)}, u32[]{:S(2)}) async-start(bf16[8,512,256]{2,1,0:T(8,128)(2,1)} %bitcast.43), calls=%async_computation.3 | async-start | bytes 4194304 | tf_op jit(solution)/shard_map/all_to_all | solution.py:190
  267.8 1.2 copy-done.5
  269.0 14.7 %attend.6.refs_4_ = bf16[768,256]{1,0:T(8,128)(2,1)} custom-call(s32[192]{0:T(256)S(1)} %fusion.14.place_ref, bf16[768,640]{1,0:T(8,128)(2,1)S(1)} %copy-done.5, bf16[768,640]{1,0:T(8,128)(2,1)S(1)} %copy-done.5, bf16[4096,512]{1,0:T(8,128)(2,1)} %bitcast.7.refs_2_.refs_3_, bf16[4096,512]{1,0:T(8,128)(2,1)} %bitcast.7.refs_2_.refs_3_), custom_call_target="tpu_custom_call" | custom-call | flops 805306368 | bytes 4194304 | tf_op jit(solution)/shard_map/attend/pallas_call | solution.py:97
  283.7 0.9 collective-permute-start.20
  284.5 3.5 %collective-permute-start.21 = (bf16[768,256]{1,0:T(8,128)(2,1)}, bf16[768,256]{1,0:T(8,128)(2,1)}, u32[]{:S(2)}, u32[]{:S(2)}) collective-permute-start(bf16[768,256]{1,0:T(8,128)(2,1)} %attend.6.refs_4_), channel_id=1, source_target_pairs={{0,2},{1,3},{2,0},{3,1},{4,6},{5,7},{6,4},{7,5},{8,10},{9,11},{10,... | collective-permute-start | bytes 1179656 | tf_op jit(solution)/shard_map/ppermute | solution.py:221
  288.1 6.2 %all-to-all-done.3 = bf16[8,512,256]{2,1,0:T(8,128)(2,1)} async-done(((bf16[8,512,256]{2,1,0:T(8,128)(2,1)}), bf16[8,512,256]{2,1,0:T(8,128)(2,1)}, u32[]{:S(2)}, u32[]{:S(2)}) %all-to-all-start.3) | async-done | bytes 2097184 | tf_op jit(solution)/shard_map/all_to_all | solution.py:190
  294.2 1.3 copy-done.6
  295.6 7.8 %attend.7.refs_0_ = bf16[768,128]{1,0:T(8,128)(2,1)S(1)} custom-call(s32[192]{0:T(256)S(1)} %fusion.14.place_ref, bf16[768,640]{1,0:T(8,128)(2,1)S(1)} %copy-done.6, bf16[4096,256]{1,0:T(8,128)(2,1)} %bitcast.9.refs_1_), custom_call_target="tpu_custom_call" | custom-call | flops 402653184 | bytes 2097152 | tf_op jit(solution)/shard_map/attend/pallas_call | solution.py:97
  303.4 0.9 collective-permute-start.17
  304.3 3.5 %collective-permute-start.18 = (bf16[768,128]{1,0:T(8,128)(2,1)S(1)}, bf16[768,128]{1,0:T(8,128)(2,1)S(1)}, u32[]{:S(2)}, u32[]{:S(2)}) collective-permute-start(bf16[768,128]{1,0:T(8,128)(2,1)S(1)} %attend.7.refs_0_), channel_id=1, source_target_pairs={{0,2},{1,3},{2,0},{3,1},{4,6},{5,7},{6,4},{7,5},{8,10},{9,11},{10,... | collective-permute-start | bytes 589832 | tf_op jit(solution)/shard_map/ppermute | solution.py:221
  307.9 8.1 %project.2.refs_8_ = f32[768,1280]{1,0:T(8,128)S(1)} custom-call(bf16[768,128]{1,0:T(8,128)(2,1)S(1)} %attend.4.refs_0_, bf16[768,128]{1,0:T(8,128)(2,1)S(1)} %copy-done.17, bf16[768,128]{1,0:T(8,128)(2,1)S(1)} %copy-done.19, bf16[768,128]{1,0:T(8,128)(2,1)S(1)} %copy-done.15, bf16[768,256]{1,0:T(8,128)(2,1)} %attend.6.refs_4_, ...), custom_call_target="tpu_custom_call" | custom-call | flops 4026531840 | bytes 10354688 | tf_op jit(solution)/shard_map/project/pallas_call | solution.py:156
  316.2 4.8 %project.3 = bf16[768,1280]{1,0:T(8,128)(2,1)} custom-call(bf16[768,128]{1,0:T(8,128)(2,1)S(1)} %attend.7.refs_0_, bf16[768,128]{1,0:T(8,128)(2,1)S(1)} %collective-permute-done.17.refs_1_, bf16[768,128]{1,0:T(8,128)(2,1)S(1)} %collective-permute-done.18.refs_2_, bf16[768,128]{1,0:T(8,128)(2,1)S(1)} %collective-permute-done.19.refs_3_, ...), custom_call_target="tpu_custom_call" | custom-call | flops 1006632960 | bytes 4063232 | tf_op jit(solution)/shard_map/project/pallas_call | solution.py:156
  (92 shorter events, 9.3 us)
Async XLA Ops:
  6.5 52.3 %all-gather.8.cloned.1.call-start = ((), (), s32[]{:S(2)}) async-start(), calls=%async_computation.4 | async-start | bytes 3538944 | tf_op jit(solution)/shard_map/all_gather | solution.py:225
  7.9 3.3 copy-start.23
  7.9 3.3 copy-start.24
  10.1 192.0 %all-gather.10.cloned.1.call-start = ((), (), s32[]{:S(2)}) async-start(), calls=%async_computation.5 | async-start | bytes 7077888 | tf_op jit(solution)/shard_map/all_gather | solution.py:225
  58.8 1.9 copy-start.13
  61.5 1.4 copy-start.8
  62.9 10.9 %collective-permute-start = (bf16[768,256]{1,0:T(8,128)(2,1)S(1)}, bf16[768,256]{1,0:T(8,128)(2,1)S(1)}, u32[]{:S(2)}, u32[]{:S(2)}) collective-permute-start(bf16[768,256]{1,0:T(8,128)(2,1)S(1)} %get-tuple-element.31), channel_id=1, source_target_pairs={{0,8},{8,16},{16,24},{24,32},{32,40},{40,48},{48,56},{56,0},{1,9},... | collective-permute-start | bytes 1179656 | tf_op jit(solution)/shard_map/ppermute | solution.py:234
  62.9 11.8 %collective-permute-start.4 = (bf16[768,256]{1,0:T(8,128)(2,1)S(1)}, bf16[768,256]{1,0:T(8,128)(2,1)S(1)}, u32[]{:S(2)}, u32[]{:S(2)}) collective-permute-start(bf16[768,256]{1,0:T(8,128)(2,1)S(1)} %get-tuple-element.31), channel_id=1, source_target_pairs={{0,56},{8,0},{16,8},{24,16},{32,24},{40,32},{48,40},{56,48},{1,57}... | collective-permute-start | bytes 1179656 | tf_op jit(solution)/shard_map/ppermute | solution.py:235
  65.6 64.2 %all-to-all-start = ((bf16[8,512,256]{2,1,0:T(8,128)(2,1)}), bf16[8,512,256]{2,1,0:T(8,128)(2,1)S(1)}, u32[]{:S(2)}, u32[]{:S(2)}) async-start(bf16[8,512,256]{2,1,0:T(8,128)(2,1)} %bitcast.42), calls=%async_computation | async-start | bytes 4194304 | tf_op jit(solution)/shard_map/all_to_all | solution.py:190
  71.3 158.2 %all-gather.12.cloned.1.call-start = ((), (), s32[]{:S(2)}) async-start(), calls=%async_computation.6 | async-start | bytes 3538944 | tf_op jit(solution)/shard_map/all_gather | solution.py:225
  73.8 23.7 %copy-start.22 = (bf16[768,256]{1,0:T(8,128)(2,1)}, bf16[768,256]{1,0:T(8,128)(2,1)S(1)}, u32[]{:S(2)}) copy-start(bf16[768,256]{1,0:T(8,128)(2,1)S(1)} %collective-permute-done) | copy-start | bytes 1179652
  73.8 19.7 %collective-permute-start.1 = (bf16[768,256]{1,0:T(8,128)(2,1)S(1)}, bf16[768,256]{1,0:T(8,128)(2,1)}, u32[]{:S(2)}, u32[]{:S(2)}) collective-permute-start(bf16[768,256]{1,0:T(8,128)(2,1)S(1)} %collective-permute-done), channel_id=1, source_target_pairs={{0,8},{8,16},{16,24},{24,32},{32,40},{40,48},{48,56},{56,0},{1,9},... | collective-permute-start | bytes 1179656 | tf_op jit(solution)/shard_map/ppermute | solution.py:234
  74.7 23.0 %copy-start.20 = (bf16[768,256]{1,0:T(8,128)(2,1)}, bf16[768,256]{1,0:T(8,128)(2,1)S(1)}, u32[]{:S(2)}) copy-start(bf16[768,256]{1,0:T(8,128)(2,1)S(1)} %collective-permute-done.4) | copy-start | bytes 1179652
  74.7 19.3 %collective-permute-start.5 = (bf16[768,256]{1,0:T(8,128)(2,1)S(1)}, bf16[768,256]{1,0:T(8,128)(2,1)}, u32[]{:S(2)}, u32[]{:S(2)}) collective-permute-start(bf16[768,256]{1,0:T(8,128)(2,1)S(1)} %collective-permute-done.4), channel_id=1, source_target_pairs={{0,56},{8,0},{16,8},{24,16},{32,24},{40,32},{48,40},{56,48},{1,57}... | collective-permute-start | bytes 1179656 | tf_op jit(solution)/shard_map/ppermute | solution.py:235
  93.6 19.7 %collective-permute-start.2 = (bf16[768,256]{1,0:T(8,128)(2,1)}, bf16[768,256]{1,0:T(8,128)(2,1)}, u32[]{:S(2)}, u32[]{:S(2)}) collective-permute-start(bf16[768,256]{1,0:T(8,128)(2,1)} %collective-permute-done.1), channel_id=1, source_target_pairs={{0,8},{8,16},{16,24},{24,32},{32,40},{40,48},{48,56},{56,0},{1,9},... | collective-permute-start | bytes 1179656 | tf_op jit(solution)/shard_map/ppermute | solution.py:234
  93.9 21.4 %collective-permute-start.6 = (bf16[768,256]{1,0:T(8,128)(2,1)}, bf16[768,256]{1,0:T(8,128)(2,1)}, u32[]{:S(2)}, u32[]{:S(2)}) collective-permute-start(bf16[768,256]{1,0:T(8,128)(2,1)} %collective-permute-done.5), channel_id=1, source_target_pairs={{0,56},{8,0},{16,8},{24,16},{32,24},{40,32},{48,40},{56,48},{1,57}... | collective-permute-start | bytes 1179656 | tf_op jit(solution)/shard_map/ppermute | solution.py:235
  97.7 30.4 %copy-start.21 = (bf16[768,256]{1,0:T(8,128)(2,1)S(1)}, bf16[768,256]{1,0:T(8,128)(2,1)}, u32[]{:S(2)}) copy-start(bf16[768,256]{1,0:T(8,128)(2,1)} %copy-done.20) | copy-start | bytes 1179652
  97.7 32.1 %copy-start.3 = (bf16[768,640]{1,0:T(8,128)(2,1)S(1)}, bf16[768,640]{1,0:T(8,128)(2,1)}, u32[]{:S(2)}) copy-start(bf16[768,640]{1,0:T(8,128)(2,1)} %refs_0_.7) | copy-start | bytes 2949124
  114.2 10.8 %collective-permute-start.3 = (bf16[384,256]{1,0:T(8,128)(2,1)S(1)}, bf16[384,256]{1,0:T(8,128)(2,1)S(1)}, u32[]{:S(2)}, u32[]{:S(2)}) collective-permute-start(bf16[384,256]{1,0:T(8,128)(2,1)S(1)} %slice.48), channel_id=1, source_target_pairs={{0,8},{8,16},{16,24},{24,32},{32,40},{40,48},{48,56},{56,0},{1,9},... | collective-permute-start | bytes 589832 | tf_op jit(solution)/shard_map/ppermute | solution.py:234
  116.3 9.7 %collective-permute-start.7 = (bf16[384,256]{1,0:T(8,128)(2,1)S(1)}, bf16[384,256]{1,0:T(8,128)(2,1)S(1)}, u32[]{:S(2)}, u32[]{:S(2)}) collective-permute-start(bf16[384,256]{1,0:T(8,128)(2,1)S(1)} %slice.49), channel_id=1, source_target_pairs={{0,56},{8,0},{16,8},{24,16},{32,24},{40,32},{48,40},{56,48},{1,57}... | collective-permute-start | bytes 589832 | tf_op jit(solution)/shard_map/ppermute | solution.py:235
  128.1 1.7 copy-start.10
  129.8 6.2 %copy-start.11 = (bf16[6144,256]{1,0:T(8,128)(2,1)S(1)}, bf16[6144,256]{1,0:T(8,128)(2,1)}, u32[]{:S(2)}) copy-start(bf16[6144,256]{1,0:T(8,128)(2,1)} %copy-done.10) | copy-start | bytes 9437188
  138.0 70.4 %all-to-all-start.1 = ((bf16[8,512,256]{2,1,0:T(8,128)(2,1)}), bf16[8,512,256]{2,1,0:T(8,128)(2,1)}, u32[]{:S(2)}, u32[]{:S(2)}) async-start(bf16[8,512,256]{2,1,0:T(8,128)(2,1)} %bitcast.4), calls=%async_computation.1 | async-start | bytes 4194304 | tf_op jit(solution)/shard_map/all_to_all | solution.py:190
  153.6 38.6 %collective-permute-start.11 = (bf16[640,1280]{1,0:T(8,128)(2,1)S(1)}, bf16[640,1280]{1,0:T(8,128)(2,1)S(1)}, u32[]{:S(2)}, u32[]{:S(2)}) collective-permute-start(bf16[640,1280]{1,0:T(8,128)(2,1)S(1)} %get-tuple-element.55), channel_id=1, source_target_pairs={{0,1},{1,2},{2,3},{3,0},{4,5},{5,6},{6,7},{7,4},{8,9},{9,10},{10,1... | collective-permute-start | bytes 4915208 | tf_op jit(solution)/shard_map/ppermute | solution.py:218
  154.7 37.4 %collective-permute-start.12 = (bf16[640,1280]{1,0:T(8,128)(2,1)S(1)}, bf16[640,1280]{1,0:T(8,128)(2,1)S(1)}, u32[]{:S(2)}, u32[]{:S(2)}) collective-permute-start(bf16[640,1280]{1,0:T(8,128)(2,1)S(1)} %get-tuple-element.54), channel_id=1, source_target_pairs={{0,3},{1,0},{2,1},{3,2},{4,7},{5,4},{6,5},{7,6},{8,11},{9,8},{10,9... | collective-permute-start | bytes 4915208 | tf_op jit(solution)/shard_map/ppermute | solution.py:218
  156.3 39.8 %collective-permute-start.10 = (bf16[768,128]{1,0:T(8,128)(2,1)S(1)}, bf16[768,128]{1,0:T(8,128)(2,1)S(1)}, u32[]{:S(2)}, u32[]{:S(2)}) collective-permute-start(bf16[768,128]{1,0:T(8,128)(2,1)S(1)} %attend.4.refs_0_), channel_id=1, source_target_pairs={{0,3},{1,0},{2,1},{3,2},{4,7},{5,4},{6,5},{7,6},{8,11},{9,8},{10,9... | collective-permute-start | bytes 589832 | tf_op jit(solution)/shard_map/ppermute | solution.py:221
  157.4 39.3 %collective-permute-start.8 = (bf16[768,128]{1,0:T(8,128)(2,1)S(1)}, bf16[768,128]{1,0:T(8,128)(2,1)S(1)}, u32[]{:S(2)}, u32[]{:S(2)}) collective-permute-start(bf16[768,128]{1,0:T(8,128)(2,1)S(1)} %attend.4.refs_0_), channel_id=1, source_target_pairs={{0,1},{1,2},{2,3},{3,0},{4,5},{5,6},{6,7},{7,4},{8,9},{9,10},{10,1... | collective-permute-start | bytes 589832 | tf_op jit(solution)/shard_map/ppermute | solution.py:221
  157.8 43.7 %collective-permute-start.9 = (bf16[768,128]{1,0:T(8,128)(2,1)S(1)}, bf16[768,128]{1,0:T(8,128)(2,1)S(1)}, u32[]{:S(2)}, u32[]{:S(2)}) collective-permute-start(bf16[768,128]{1,0:T(8,128)(2,1)S(1)} %attend.4.refs_0_), channel_id=1, source_target_pairs={{0,2},{1,3},{2,0},{3,1},{4,6},{5,7},{6,4},{7,5},{8,10},{9,11},{10,... | collective-permute-start | bytes 589832 | tf_op jit(solution)/shard_map/ppermute | solution.py:221
  192.2 1.2 copy-start
  196.1 0.7 copy-start.14
  196.8 0.7 copy-start.16
  201.5 0.7 copy-start.18
  202.1 2.8 copy-start.2
  206.4 2.0 copy-start.7
  208.4 54.2 %all-to-all-start.2 = ((bf16[8,512,512]{2,1,0:T(8,128)(2,1)}), bf16[8,512,512]{2,1,0:T(8,128)(2,1)}, u32[]{:S(2)}, u32[]{:S(2)}) async-start(bf16[8,512,512]{2,1,0:T(8,128)(2,1)} %bitcast.40), calls=%async_computation.2 | async-start | bytes 8388608 | tf_op jit(solution)/shard_map/all_to_all | solution.py:190
  213.7 39.0 %collective-permute-start.13 = (bf16[640,1280]{1,0:T(8,128)(2,1)}, bf16[640,1280]{1,0:T(8,128)(2,1)}, u32[]{:S(2)}, u32[]{:S(2)}) collective-permute-start(bf16[640,1280]{1,0:T(8,128)(2,1)} %get-tuple-element.56), channel_id=1, source_target_pairs={{0,2},{1,3},{2,0},{3,1},{4,6},{5,7},{6,4},{7,5},{8,10},{9,11},{10,... | collective-permute-start | bytes 4915208 | tf_op jit(solution)/shard_map/ppermute | solution.py:218
  214.3 1.2 copy-start.4
  223.9 34.1 %collective-permute-start.14 = (bf16[768,128]{1,0:T(8,128)(2,1)}, bf16[768,128]{1,0:T(8,128)(2,1)}, u32[]{:S(2)}, u32[]{:S(2)}) collective-permute-start(bf16[768,128]{1,0:T(8,128)(2,1)} %attend.5.refs_8_), channel_id=1, source_target_pairs={{0,1},{1,2},{2,3},{3,0},{4,5},{5,6},{6,7},{7,4},{8,9},{9,10},{10,1... | collective-permute-start | bytes 589832 | tf_op jit(solution)/shard_map/ppermute | solution.py:221
  227.2 34.0 %collective-permute-start.15 = (bf16[768,128]{1,0:T(8,128)(2,1)}, bf16[768,128]{1,0:T(8,128)(2,1)}, u32[]{:S(2)}, u32[]{:S(2)}) collective-permute-start(bf16[768,128]{1,0:T(8,128)(2,1)} %attend.5.refs_8_), channel_id=1, source_target_pairs={{0,2},{1,3},{2,0},{3,1},{4,6},{5,7},{6,4},{7,5},{8,10},{9,11},{10,... | collective-permute-start | bytes 589832 | tf_op jit(solution)/shard_map/ppermute | solution.py:221
  227.8 34.3 %collective-permute-start.16 = (bf16[768,128]{1,0:T(8,128)(2,1)}, bf16[768,128]{1,0:T(8,128)(2,1)}, u32[]{:S(2)}, u32[]{:S(2)}) collective-permute-start(bf16[768,128]{1,0:T(8,128)(2,1)} %attend.5.refs_8_), channel_id=1, source_target_pairs={{0,3},{1,0},{2,1},{3,2},{4,7},{5,4},{6,5},{7,6},{8,11},{9,8},{10,9... | collective-permute-start | bytes 589832 | tf_op jit(solution)/shard_map/ppermute | solution.py:221
  229.6 1.9 copy-start.12
  232.2 1.3 copy-start.9
  262.7 31.6 %all-to-all-start.3 = ((bf16[8,512,256]{2,1,0:T(8,128)(2,1)}), bf16[8,512,256]{2,1,0:T(8,128)(2,1)}, u32[]{:S(2)}, u32[]{:S(2)}) async-start(bf16[8,512,256]{2,1,0:T(8,128)(2,1)} %bitcast.43), calls=%async_computation.3 | async-start | bytes 4194304 | tf_op jit(solution)/shard_map/all_to_all | solution.py:190
  267.8 1.2 copy-start.5
  283.7 24.2 %collective-permute-start.20 = (bf16[768,256]{1,0:T(8,128)(2,1)}, bf16[768,256]{1,0:T(8,128)(2,1)}, u32[]{:S(2)}, u32[]{:S(2)}) collective-permute-start(bf16[768,256]{1,0:T(8,128)(2,1)} %attend.6.refs_4_), channel_id=1, source_target_pairs={{0,1},{1,2},{2,3},{3,0},{4,5},{5,6},{6,7},{7,4},{8,9},{9,10},{10,1... | collective-permute-start | bytes 1179656 | tf_op jit(solution)/shard_map/ppermute | solution.py:221
  284.5 23.3 %collective-permute-start.21 = (bf16[768,256]{1,0:T(8,128)(2,1)}, bf16[768,256]{1,0:T(8,128)(2,1)}, u32[]{:S(2)}, u32[]{:S(2)}) collective-permute-start(bf16[768,256]{1,0:T(8,128)(2,1)} %attend.6.refs_4_), channel_id=1, source_target_pairs={{0,2},{1,3},{2,0},{3,1},{4,6},{5,7},{6,4},{7,5},{8,10},{9,11},{10,... | collective-permute-start | bytes 1179656 | tf_op jit(solution)/shard_map/ppermute | solution.py:221
  288.1 19.8 %collective-permute-start.22 = (bf16[768,256]{1,0:T(8,128)(2,1)}, bf16[768,256]{1,0:T(8,128)(2,1)}, u32[]{:S(2)}, u32[]{:S(2)}) collective-permute-start(bf16[768,256]{1,0:T(8,128)(2,1)} %attend.6.refs_4_), channel_id=1, source_target_pairs={{0,3},{1,0},{2,1},{3,2},{4,7},{5,4},{6,5},{7,6},{8,11},{9,8},{10,9... | collective-permute-start | bytes 1179656 | tf_op jit(solution)/shard_map/ppermute | solution.py:221
  294.2 13.6 %copy-start.1 = (bf16[640,1280]{1,0:T(8,128)(2,1)S(1)}, bf16[640,1280]{1,0:T(8,128)(2,1)}, u32[]{:S(2)}) copy-start(bf16[640,1280]{1,0:T(8,128)(2,1)} %copy-done) | copy-start | bytes 4915204
  294.2 1.3 copy-start.6
  295.5 12.3 %copy-start.15 = (bf16[768,128]{1,0:T(8,128)(2,1)S(1)}, bf16[768,128]{1,0:T(8,128)(2,1)}, u32[]{:S(2)}) copy-start(bf16[768,128]{1,0:T(8,128)(2,1)} %copy-done.14) | copy-start | bytes 589828
  295.6 12.3 %copy-start.17 = (bf16[768,128]{1,0:T(8,128)(2,1)S(1)}, bf16[768,128]{1,0:T(8,128)(2,1)}, u32[]{:S(2)}) copy-start(bf16[768,128]{1,0:T(8,128)(2,1)} %copy-done.16) | copy-start | bytes 589828
  295.6 12.3 %copy-start.19 = (bf16[768,128]{1,0:T(8,128)(2,1)S(1)}, bf16[768,128]{1,0:T(8,128)(2,1)}, u32[]{:S(2)}) copy-start(bf16[768,128]{1,0:T(8,128)(2,1)} %copy-done.18) | copy-start | bytes 589828
  303.4 12.7 %collective-permute-start.17 = (bf16[768,128]{1,0:T(8,128)(2,1)S(1)}, bf16[768,128]{1,0:T(8,128)(2,1)S(1)}, u32[]{:S(2)}, u32[]{:S(2)}) collective-permute-start(bf16[768,128]{1,0:T(8,128)(2,1)S(1)} %attend.7.refs_0_), channel_id=1, source_target_pairs={{0,1},{1,2},{2,3},{3,0},{4,5},{5,6},{6,7},{7,4},{8,9},{9,10},{10,1... | collective-permute-start | bytes 589832 | tf_op jit(solution)/shard_map/ppermute | solution.py:221
  304.3 11.9 %collective-permute-start.18 = (bf16[768,128]{1,0:T(8,128)(2,1)S(1)}, bf16[768,128]{1,0:T(8,128)(2,1)S(1)}, u32[]{:S(2)}, u32[]{:S(2)}) collective-permute-start(bf16[768,128]{1,0:T(8,128)(2,1)S(1)} %attend.7.refs_0_), channel_id=1, source_target_pairs={{0,2},{1,3},{2,0},{3,1},{4,6},{5,7},{6,4},{7,5},{8,10},{9,11},{10,... | collective-permute-start | bytes 589832 | tf_op jit(solution)/shard_map/ppermute | solution.py:221
  307.8 8.3 %collective-permute-start.19 = (bf16[768,128]{1,0:T(8,128)(2,1)S(1)}, bf16[768,128]{1,0:T(8,128)(2,1)S(1)}, u32[]{:S(2)}, u32[]{:S(2)}) collective-permute-start(bf16[768,128]{1,0:T(8,128)(2,1)S(1)} %attend.7.refs_0_), channel_id=1, source_target_pairs={{0,3},{1,0},{2,1},{3,2},{4,7},{5,4},{6,5},{7,6},{8,11},{9,8},{10,9... | collective-permute-start | bytes 589832 | tf_op jit(solution)/shard_map/ppermute | solution.py:221
Sparse Core Ops, SparseCore 0:
  10.3 48.5 all-gather.7
  60.6 95.2 all-gather.9
  157.7 43.4 all-gather.11
